TPU v7x, 32 devices: a whole 2x2x4 slice. The times are simulated.
32 devices in a mesh: win: 8 (over z, x), ffn: 4 (over y, core).
Axes of the slice: x: 2, y: 2, z: 4, core: 2. Of those that a mesh axis runs over, the one named last changes fastest.
Arguments:
- pillar_feats: float32 [27648, 128], P(('win', 'ffn')), may hold values from -40 to 40
- occupied: int32 [27648], P(('win', 'ffn')), may hold values from 0 to 1, as said below
- shifted_source_rows: int32 [27648], P(('win', 'ffn')), may hold values from 0 to 27647, as said below
- w_vfe: float32 [128, 128], replicated, may hold values from -0.5 to 0.5
- bn_gain: float32 [2, 128], replicated, may hold values from 0.5 to 1.5
- bn_shift: float32 [2, 128], replicated, may hold values from -3 to 3
- query_key_value_weight: float32 [2, 128, 384], replicated, may hold values from -0.75 to 0.75
- attention_output_weight: float32 [2, 128, 128], replicated, may hold values from -1 to 1
- up_weight_matrix: float32 [2, 128, 256], P(None, None, 'ffn'), may hold values from -0.5 to 0.5
- up_bias_rows: float32 [2, 256], P(None, 'ffn'), may hold values from -3 to 3
- down_weight_matrix: float32 [2, 256, 128], P(None, 'ffn'), may hold values from -0.375 to 0.375
- down_bias_rows: float32 [2, 128], replicated, may hold values from -3 to 3
- layernorm_gains: float32 [4, 128], replicated, may hold values from 0.5 to 1.5
- layernorm_offsets: float32 [4, 128], replicated, may hold values from -3 to 3
- cotangent: float32 [27648, 128], P(('win', 'ffn')), may hold values from -6 to 6
Outputs:
- pillars_out: float32 [27648, 128], P(('win', 'ffn'))
- grad_pillar_feats: float32 [27648, 128], P(('win', 'ffn'))
- grad_w_vfe: float32 [128, 128], replicated
- grad_bn_gain: float32 [2, 128], replicated
- grad_bn_shift: float32 [2, 128], replicated
- grad_w_qkv: float32 [2, 128, 384], replicated
- grad_w_out: float32 [2, 128, 128], replicated
- grad_w_in: float32 [2, 128, 256], P(None, None, 'ffn')
- grad_b_in: float32 [2, 256], P(None, 'ffn')
- grad_w_back: float32 [2, 256, 128], P(None, 'ffn')
- grad_b_back: float32 [2, 128], replicated
- grad_ln_gain: float32 [4, 128], replicated
- grad_ln_shift: float32 [4, 128], replicated
Inputs may be any that keep to these rules, and one draw needn't show every extreme that they name: Every window of 144 consecutive rows has from 36 to 144 occupied slots; both counts occur in every draw. `shifted_source_rows`: A permutation of the 27648 rows. With g = t // 864, row t takes a regular row from g * 864 + 72 to g * 864 + 935, counted modulo 27648; which of these rows fall into which shifted window is arbitrary.
All inputs are finite; a program needn't handle non-finite values.
Results may differ from a plain program's by a relative error of at most 0.0003.
Values sent between devices are 32-bit elements; how exact they have to be, the bound alone decides.
No kernel may reach another device: no remote copies, remote signals or barrier semaphores. Data moves between devices by JAX's collectives and lax.ppermute only.
A program may use at most 128 MiB of HBM per device.

v0:
```python
import math

import jax
import jax.numpy as jnp
from jax import lax
from jax.sharding import PartitionSpec as P

HEADS = 8
CELLS = 144


EPS_NORM = 1e-05
NEG_FILL = -1000000000.0


def passed_along(shard, axis, by):
    peers = lax.axis_size(axis)
    return lax.ppermute(shard, axis, [(i, (i + by) % peers) for i in range(peers)])


def matmul(former, latter):
    return jnp.dot(former, latter, precision=lax.Precision.HIGHEST)


def outer_sum(former, latter):
    return lax.dot_general(
        former, latter, (((0,), (0,)), ((), ())), precision=lax.Precision.HIGHEST
    )


def back_product(former, latter):
    return lax.dot_general(
        former, latter, (((1,), (1,)), ((), ())), precision=lax.Precision.HIGHEST
    )


def gelu_exact(values):
    return jax.nn.gelu(values, approximate=False)


def layer_norm(values, norm_gain, norm_shift):
    center = jnp.mean(values, axis=-1, keepdims=True)
    spread = jnp.mean((values - center) ** 2, axis=-1, keepdims=True)
    return (values - center) * lax.rsqrt(spread + EPS_NORM) * norm_gain + norm_shift


def window_core(window_rows, key_live, w_qkv_one):
    windows, window_cells, model_width = window_rows.shape
    head_width = model_width // HEADS
    packed = jnp.einsum("wcd,de->wce", window_rows, w_qkv_one, precision=lax.Precision.HIGHEST)
    queries = packed[..., :model_width].reshape(windows, window_cells, HEADS, head_width)
    key_rows = packed[..., model_width : 2 * model_width].reshape(
        windows, window_cells, HEADS, head_width
    )
    value_rows = packed[..., 2 * model_width :].reshape(windows, window_cells, HEADS, head_width)
    scores = jnp.einsum(
        "wqhe,wkhe->whqk", queries, key_rows, precision=lax.Precision.HIGHEST
    ) / math.sqrt(head_width)
    scores = jnp.where(key_live[:, None, None, :] > 0, scores, NEG_FILL)
    scores = scores - jnp.max(scores, axis=-1, keepdims=True)
    weights = jnp.exp(scores)
    weights = weights / jnp.sum(weights, axis=-1, keepdims=True)
    mixture = jnp.einsum("whqk,wkhe->wqhe", weights, value_rows, precision=lax.Precision.HIGHEST)
    return mixture.reshape(windows, window_cells, model_width)


def norm_stats(values, live_rows):
    col_total, rows_live = lax.psum(
        (jnp.sum(live_rows * values, axis=0), jnp.sum(live_rows)), ("win", "ffn")
    )
    center = col_total / rows_live
    spread = (
        lax.psum(jnp.sum(live_rows * (values - center) ** 2, axis=0), ("win", "ffn")) / rows_live
    )
    return (center, lax.rsqrt(spread + EPS_NORM), rows_live)


def norm_back(grad_output, normed_hat, live_rows, stats, norm_gain):
    gain_grad, shift_grad = lax.psum(
        (jnp.sum(grad_output * normed_hat, axis=0), jnp.sum(grad_output, axis=0)), ("win", "ffn")
    )
    grad_values = (
        stats[1]
        * norm_gain
        * (grad_output - live_rows * (normed_hat * gain_grad + shift_grad) / stats[2])
    )
    return (grad_values, gain_grad, shift_grad)


def local_rows(source, row_count):
    devices = lax.axis_size(("win", "ffn"))
    return (source - lax.axis_index(("win", "ffn")) * row_count) % (row_count * devices)


def to_shifted(values, live_rows, source):
    row_count = values.shape[0]
    half_window = CELLS // 2
    incoming, incoming_live = passed_along(
        (values[:half_window], live_rows[:half_window]), ("win", "ffn"), -1
    )
    places = local_rows(source, row_count)
    return (
        jnp.concatenate([values, incoming])[places],
        jnp.concatenate([live_rows, incoming_live])[places],
    )


def to_regular(values, source):
    row_count = values.shape[0]
    half_window = CELLS // 2
    places = local_rows(source, row_count)
    placed_rows = (
        jnp.zeros((row_count + half_window, values.shape[1]), values.dtype).at[places].set(values)
    )
    incoming = passed_along(placed_rows[row_count:], ("win", "ffn"), 1)
    return jnp.concatenate([incoming, placed_rows[half_window:row_count]])


def ffn_forward(first_norm, in_one, bias_one, back_one):
    gathered = lax.all_gather(first_norm, "ffn", axis=0, tiled=True)
    hidden, pull_hidden = jax.vjp(gelu_exact, matmul(gathered, in_one) + bias_one)
    ffn_out = lax.psum_scatter(matmul(hidden, back_one), "ffn", scatter_dimension=0, tiled=True)
    return (ffn_out, (gathered, hidden, pull_hidden))


def ffn_backward(grad_output, ffn_keep, in_one, back_one):
    gathered, hidden, pull_hidden = ffn_keep
    grad_rows = lax.all_gather(grad_output, "ffn", axis=0, tiled=True)
    grad_pre = pull_hidden(back_product(grad_rows, back_one))[0]
    ffn_grads = (
        outer_sum(gathered, grad_pre),
        jnp.sum(grad_pre, axis=0),
        outer_sum(hidden, grad_rows),
    )
    grad_first = lax.psum_scatter(
        back_product(grad_pre, in_one), "ffn", scatter_dimension=0, tiled=True
    )
    return (grad_first, ffn_grads)


def layer_forward(
    carried_state,
    live_rows,
    layer_picker,
    query_key_value_weight,
    attention_output_weight,
    ffn_in,
    ffn_bias,
    ffn_back,
    down_bias_rows,
    layernorm_gains,
    layernorm_offsets,
):
    key_live = live_rows[:, 0].reshape(-1, CELLS)

    def front_part(values, qkv_one, out_one, norm_gain, norm_shift):
        window_rows = values.reshape(-1, CELLS, values.shape[-1])
        mixture = window_core(window_rows, key_live, qkv_one).reshape(values.shape)
        return layer_norm(values + matmul(mixture, out_one), norm_gain, norm_shift)

    first_norm, pull_front = jax.vjp(
        front_part,
        carried_state,
        query_key_value_weight[layer_picker],
        attention_output_weight[layer_picker],
        layernorm_gains[2 * layer_picker],
        layernorm_offsets[2 * layer_picker],
    )
    ffn_out, ffn_keep = ffn_forward(
        first_norm, ffn_in[layer_picker], ffn_bias[layer_picker], ffn_back[layer_picker]
    )
    second_norm, pull_second = jax.vjp(
        layer_norm,
        first_norm + ffn_out + down_bias_rows[layer_picker],
        layernorm_gains[2 * layer_picker + 1],
        layernorm_offsets[2 * layer_picker + 1],
    )
    return (second_norm, (pull_front, ffn_keep, pull_second))


def layer_backward(grad_second, layer_keep, layer_picker, ffn_in, ffn_back):
    pull_front, ffn_keep, pull_second = layer_keep
    grad_summed, gain_two, shift_two = pull_second(grad_second)
    grad_first_ffn, ffn_grads = ffn_backward(
        grad_summed, ffn_keep, ffn_in[layer_picker], ffn_back[layer_picker]
    )
    grad_carried, grad_qkv, grad_out_proj, gain_one, shift_one = pull_front(
        grad_summed + grad_first_ffn
    )
    return (
        grad_carried,
        (
            grad_qkv,
            grad_out_proj,
            ffn_grads[0],
            ffn_grads[1],
            ffn_grads[2],
            jnp.sum(grad_summed, axis=0),
            gain_one,
            gain_two,
            shift_one,
            shift_two,
        ),
    )


def on_device(
    pillar_feats,
    occupied,
    shifted_source_rows,
    w_vfe,
    bn_gain,
    bn_shift,
    query_key_value_weight,
    attention_output_weight,
    up_weight_matrix,
    up_bias_rows,
    down_weight_matrix,
    down_bias_rows,
    layernorm_gains,
    layernorm_offsets,
    cotangent,
):
    live_rows = occupied.astype(jnp.float32)[:, None]
    ffn_in, ffn_bias, ffn_back = (up_weight_matrix, up_bias_rows, down_weight_matrix)
    lifted = matmul(pillar_feats, w_vfe)
    vfe_stats = norm_stats(lifted, live_rows)
    vfe_hat = (lifted - vfe_stats[0]) * vfe_stats[1]
    carried_state, pull_gelu = jax.vjp(gelu_exact, vfe_hat * bn_gain[0] + bn_shift[0])
    first_out, first_keep = layer_forward(
        carried_state,
        live_rows,
        0,
        query_key_value_weight,
        attention_output_weight,
        ffn_in,
        ffn_bias,
        ffn_back,
        down_bias_rows,
        layernorm_gains,
        layernorm_offsets,
    )
    shifted_tokens, shifted_live_mask = to_shifted(first_out, live_rows, shifted_source_rows)
    second_out, second_keep = layer_forward(
        shifted_tokens,
        shifted_live_mask,
        1,
        query_key_value_weight,
        attention_output_weight,
        ffn_in,
        ffn_bias,
        ffn_back,
        down_bias_rows,
        layernorm_gains,
        layernorm_offsets,
    )
    regular = to_regular(second_out, shifted_source_rows)
    neck_stats = norm_stats(regular, live_rows)
    neck_hat = (regular - neck_stats[0]) * neck_stats[1]
    pillars_out = live_rows * (neck_hat * bn_gain[1] + bn_shift[1])
    grad_regular, neck_gain_grad, neck_shift_grad = norm_back(
        cotangent * live_rows, neck_hat, live_rows, neck_stats, bn_gain[1]
    )
    grad_second_out, unused_live = to_shifted(grad_regular, live_rows, shifted_source_rows)
    grad_shifted, second_grads = layer_backward(grad_second_out, second_keep, 1, ffn_in, ffn_back)
    grad_first_out = to_regular(grad_shifted, shifted_source_rows)
    grad_carried, first_grads = layer_backward(grad_first_out, first_keep, 0, ffn_in, ffn_back)
    grad_affine = pull_gelu(grad_carried)[0]
    grad_lifted, vfe_gain_grad, vfe_shift_grad = norm_back(
        grad_affine, vfe_hat, live_rows, vfe_stats, bn_gain[0]
    )
    grad_pillar_feats = back_product(grad_lifted, w_vfe)
    local_w_vfe = outer_sum(pillar_feats, grad_lifted)
    stacked = [jnp.stack([first_grads[member], second_grads[member]]) for member in range(6)]
    local_ln_gain = jnp.stack([first_grads[6], first_grads[7], second_grads[6], second_grads[7]])
    local_ln_shift = jnp.stack([first_grads[8], first_grads[9], second_grads[8], second_grads[9]])
    summed = lax.psum(
        (local_w_vfe, stacked[0], stacked[1], stacked[5], local_ln_gain, local_ln_shift),
        ("win", "ffn"),
    )
    shard_in, shard_bias, shard_back = (stacked[2], stacked[3], stacked[4])
    grad_w_in, grad_b_in, grad_w_back = lax.psum((shard_in, shard_bias, shard_back), "win")
    grad_bn_gain = jnp.stack([vfe_gain_grad, neck_gain_grad])
    grad_bn_shift = jnp.stack([vfe_shift_grad, neck_shift_grad])
    return (
        pillars_out,
        grad_pillar_feats,
        summed[0],
        grad_bn_gain,
        grad_bn_shift,
        summed[1],
        summed[2],
        grad_w_in,
        grad_b_in,
        grad_w_back,
        summed[3],
        summed[4],
        summed[5],
    )


def solution(mesh):
    return jax.shard_map(
        on_device,
        mesh=mesh,
        in_specs=(
            P(("win", "ffn"), None),
            P(("win", "ffn")),
            P(("win", "ffn")),
            P(),
            P(),
            P(),
            P(),
            P(),
            P(None, None, "ffn"),
            P(None, "ffn"),
            P(None, "ffn", None),
            P(),
            P(),
            P(),
            P(("win", "ffn"), None),
        ),
        out_specs=(
            P(("win", "ffn"), None),
            P(("win", "ffn"), None),
            P(),
            P(),
            P(),
            P(),
            P(),
            P(None, None, "ffn"),
            P(None, "ffn"),
            P(None, "ffn", None),
            P(),
            P(),
            P(),
        ),
        check_vma=False,
    )
```

profile of v0, /device:TPU:0, one launch (start us, length us, event | category | flops | bytes accessed | tf_op | source)
XLA Modules:
  0.0 969.2 jit_solution(13986221595851843032)
XLA Ops:
  11.4 42.3 %all-reduce.8 = (f32[128]{0:T(128)S(1)}, f32[]{:T(128)}) all-reduce(f32[128]{0:T(128)S(1)} %get-tuple-element.124, f32[]{:T(128)} %convert_reduce_fusion.2), channel_id=1, replica_groups=mesh['win'=8,'ffn'=4] {'win','ffn'}, use_global_device_ids=true, to_apply=%region_1.0 | all-reduce | flops 129 | bytes 1032 | tf_op jit(solution)/shard_map/psum | solution.py:68
  54.6 40.3 %psum.131 = f32[128]{0:T(128)S(1)} all-reduce(f32[128]{0:T(128)S(1)} %multiply_reduce_fusion.18), channel_id=1, replica_groups=mesh['win'=8,'ffn'=4] {'win','ffn'}, use_global_device_ids=true, to_apply=%region_5.0 | all-reduce | flops 128 | bytes 1024 | tf_op jit(solution)/shard_map/psum | solution.py:73
  106.5 7.2 fusion.1
  125.8 20.6 %all-gather.5.cloned.1.call-done = f32[3456,128]{1,0:T(8,128)} async-done(((f32[864,128]{1,0:T(8,128)}), f32[3456,128]{1,0:T(8,128)}) %all-gather.5.cloned.1.call-update) | async-done | bytes 1769488 | tf_op jit(solution)/shard_map/all_gather | solution.py:120
  146.4 5.3 fusion.30
  166.4 20.3 %reduce-scatter.5.cloned.1.call-done = f32[864,128]{1,0:T(8,128)} async-done(((f32[3456,128]{1,0:T(8,128)}), f32[864,128]{1,0:T(8,128)}) %reduce-scatter.5.cloned.1.call-update) | async-done | bytes 442384 | tf_op jit(solution)/shard_map/reduce_scatter | solution.py:122
  202.1 8.4 fusion.3
  224.5 21.6 %all-gather.7.cloned.1.call-done = f32[3456,128]{1,0:T(8,128)} async-done(((f32[864,128]{1,0:T(8,128)}), f32[3456,128]{1,0:T(8,128)}) %all-gather.7.cloned.1.call-update) | async-done | bytes 1769488 | tf_op jit(solution)/shard_map/all_gather | solution.py:120
  246.1 5.3 fusion.31
  256.9 29.5 %reduce-scatter.7.cloned.1.call-done = f32[864,128]{1,0:T(8,128)} async-done(((f32[3456,128]{1,0:T(8,128)}), f32[864,128]{1,0:T(8,128)}) %reduce-scatter.7.cloned.1.call-update) | async-done | bytes 442384 | tf_op jit(solution)/shard_map/reduce_scatter | solution.py:122
  288.2 5.2 scatter_custom_fusion
  293.5 6.9 collective-permute-done.2
  301.3 37.6 %psum.132 = f32[128]{0:T(128)S(1)} all-reduce(f32[128]{0:T(128)S(1)} %multiply_reduce_fusion.13), channel_id=1, replica_groups=mesh['win'=8,'ffn'=4] {'win','ffn'}, use_global_device_ids=true, to_apply=%region_22.23 | all-reduce | flops 128 | bytes 1024 | tf_op jit(solution)/shard_map/psum | solution.py:68
  340.5 40.2 %psum.133 = f32[128]{0:T(128)S(1)} all-reduce(f32[128]{0:T(128)S(1)} %multiply_reduce_fusion.12), channel_id=1, replica_groups=mesh['win'=8,'ffn'=4] {'win','ffn'}, use_global_device_ids=true, to_apply=%region_24.25 | all-reduce | flops 128 | bytes 1024 | tf_op jit(solution)/shard_map/psum | solution.py:73
  383.3 40.1 %all-reduce.7 = (f32[128]{0:T(128)S(1)}, f32[128]{0:T(128)S(1)}) all-reduce(f32[128]{0:T(128)S(1)} %get-tuple-element.52, f32[128]{0:T(128)S(1)} %get-tuple-element.51), channel_id=1, replica_groups=mesh['win'=8,'ffn'=4] {'win','ffn'}, use_global_device_ids=true, to_apply=%region_28.29 | all-reduce | flops 256 | bytes 2048 | tf_op jit(solution)/shard_map/psum | solution.py:79
  439.1 22.0 %all-gather.9.cloned.1.call-done = f32[3456,128]{1,0:T(8,128)} async-done(((f32[864,128]{1,0:T(8,128)}), f32[3456,128]{1,0:T(8,128)}) %all-gather.9.cloned.1.call-update) | async-done | bytes 1769488 | tf_op jit(solution)/shard_map/all_gather | solution.py:128
  472.6 28.2 %reduce-scatter.9.cloned.1.call-done = f32[864,128]{1,0:T(8,128)} async-done(((f32[3456,128]{1,0:T(8,128)}), f32[864,128]{1,0:T(8,128)}) %reduce-scatter.9.cloned.1.call-update) | async-done | bytes 442384 | tf_op jit(solution)/shard_map/reduce_scatter | solution.py:135
  504.9 10.8 %fusion.26 = f32[6,8,16,144]{3,2,1,0:T(8,128)} fusion(f32[6,8,16,144]{3,2,1,0:T(8,128)S(1)} %convolution_bitcast_fusion.1, f32[6,8,144]{2,1,0:T(8,128)S(1)} %copy-done.44, f32[6,8,144,144]{2,3,1,0:T(8,128)} %copy-done.2, f32[6,8,144]{2,1,0:T(8,128)S(1)} %copy-done.40, pred[6,144]{1,0:T(8,128)(4,1)} %copy-done.73), kind=kOutput, calls=%fused_computation.47 | convolution fusion | flops 195084288 | bytes 4922208 | tf_op jit(solution)/shard_map/transpose(jvp(whqk,wkhe->wqhe))/dot_general | solution.py:63
  515.8 10.2 %convert_reduce_fusion.1 = (f32[6,8,144]{2,1,0:T(8,128)S(1)}, pred[6,8,144,144]{2,3,1,0:T(8,128)(4,1)S(1)}, f32[6,8,144]{2,1,0:T(8,128)S(1)}, f32[6,8,144,144]{2,3,1,0:T(8,128)S(1)}) fusion(f32[6,8,144]{2,1,0:T(8,128)S(1)} %copy-done.40, f32[6,8,144,144]{2,3,1,0:T(8,128)S(1)} %bitcast.244, pred[6,144]{1,0:T(8,128)(4,1)S(1)} %copy-done.74, ...), kind=kOutput, calls=%fused_computation.10 | convolution fusion | flops 200047104 | bytes 9954144 | tf_op jit(solution)/shard_map/transpose(jvp(whqk,wkhe->wqhe))/dot_general | solution.py:63
  529.5 6.1 fusion.4
  535.6 8.4 fusion.5
  555.3 5.3 scatter_custom_fusion.1
  563.0 5.3 collective-permute-done.4
  573.7 18.1 %all-gather.11.cloned.1.call-done = f32[3456,128]{1,0:T(8,128)} async-done(((f32[864,128]{1,0:T(8,128)}), f32[3456,128]{1,0:T(8,128)}) %all-gather.11.cloned.1.call-update) | async-done | bytes 1769488 | tf_op jit(solution)/shard_map/all_gather | solution.py:128
  619.5 21.9 %psum.142 = f32[2,64]{1,0:T(2,128)} all-reduce(f32[2,64]{1,0:T(2,128)S(1)} %pad_maximum_fusion.13), channel_id=1, replica_groups=mesh['win'=8,'ffn'=4] {'win'}, use_global_device_ids=true, to_apply=%region_60.61 | all-reduce | flops 128 | bytes 1024 | tf_op jit(solution)/shard_map/psum | solution.py:282
  653.8 10.6 %fusion.24 = f32[6,8,16,144]{3,2,1,0:T(8,128)} fusion(f32[6,8,16,144]{3,2,1,0:T(8,128)S(1)} %convolution_bitcast_fusion, f32[6,8,144]{2,1,0:T(8,128)} %copy-done.41, f32[6,8,144,144]{2,3,1,0:T(8,128)} %copy-done.1, f32[6,8,144]{2,1,0:T(8,128)} %copy-done.37, pred[6,144]{1,0:T(8,128)(4,1)} %copy-done.71), kind=kOutput, calls=%fused_computation.45 | convolution fusion | flops 195084288 | bytes 4922208 | tf_op jit(solution)/shard_map/transpose(jvp(whqk,wkhe->wqhe))/dot_general | solution.py:63
  664.6 10.2 %convert_reduce_fusion = (f32[6,8,144]{2,1,0:T(8,128)S(1)}, pred[6,8,144,144]{2,3,1,0:T(8,128)(4,1)S(1)}, f32[6,8,144]{2,1,0:T(8,128)S(1)}, f32[6,8,144,144]{2,3,1,0:T(8,128)S(1)}) fusion(f32[6,8,144]{2,1,0:T(8,128)S(1)} %copy-done.38, f32[6,8,144,144]{2,3,1,0:T(8,128)S(1)} %bitcast.242, pred[6,144]{1,0:T(8,128)(4,1)S(1)} %copy-done.72, ...), kind=kOutput, calls=%fused_computation.6 | convolution fusion | flops 200047104 | bytes 9954144 | tf_op jit(solution)/shard_map/transpose(jvp(whqk,wkhe->wqhe))/dot_general | solution.py:63
  678.0 6.1 fusion.6
  684.1 8.5 fusion.7
  708.0 37.0 %all-reduce.6 = (f32[128]{0:T(128)S(1)}, f32[128]{0:T(128)S(1)}, f32[2,128]{1,0:T(2,128)}, f32[4,128]{1,0:T(4,128)}, f32[4,128]{1,0:T(4,128)}) all-reduce(f32[128]{0:T(128)S(1)} %get-tuple-element.57, f32[128]{0:T(128)S(1)} %get-tuple-element.56, f32[2,128]{1,0:T(2,128)S(1)} %copy-done.87, ...), channel_id=1, replica_groups=mesh['win'=8,'ffn'=4] {'win','ffn'}, use_global_device_ids=true, to_apply=%region_53.54 | all-reduce | flops 1536 | bytes 12288 | tf_op jit(solution)/shard_map/psum | solution.py:79
  757.7 123.8 %all-reduce.14.cloned.1.call-done = (f32[128,128]{0,1:T(8,128)}, f32[2,128,384]{2,1,0:T(8,128)}, f32[2,128,128]{2,1,0:T(8,128)}) async-done(((f32[128,128]{0,1:T(8,128)}, f32[2,128,384]{2,1,0:T(8,128)}, f32[2,128,128]{2,1,0:T(8,128)}), (f32[128,128]{0,1:T(8,128)}, f32[2,128,384]{2,1,0:T(8,128)}, f32[2,128,128]{2,1,0:T(8,128)})) %all-reduce.14.cloned.1.call-update) | async-done | bytes 589840 | tf_op jit(solution)/shard_map/psum | solution.py:277
  883.1 72.7 %all-reduce.16.cloned.1.call-done = (f32[2,128,64]{1,2,0:T(8,128)}, f32[2,64,128]{2,1,0:T(8,128)}) async-done(((f32[2,128,64]{1,2,0:T(8,128)}, f32[2,64,128]{2,1,0:T(8,128)}), (f32[2,128,64]{1,2,0:T(8,128)}, f32[2,64,128]{2,1,0:T(8,128)})) %all-reduce.16.cloned.1.call-update) | async-done | bytes 131088 | tf_op jit(solution)/shard_map/psum | solution.py:282
  (408 shorter events, 217.0 us)
Async XLA Ops:
  7.2 139.2 %all-gather.5.cloned.1.call-start = ((), (), s32[]{:S(2)}) async-start(), calls=%async_computation.4 | async-start | bytes 2211840 | tf_op jit(solution)/shard_map/all_gather | solution.py:120
  10.1 105.8 %copy-start.71 = (pred[6,144]{1,0:T(8,128)(4,1)}, pred[6,144]{1,0:T(8,128)(4,1)S(1)}, u32[]{:S(2)}) copy-start(pred[6,144]{1,0:T(8,128)(4,1)S(1)} %gt.23) | copy-start | bytes 2596
  54.4 59.3 %copy-start.81 = (f32[128]{0:T(128)}, f32[128]{0:T(128)S(1)}, u32[]{:S(2)}) copy-start(f32[128]{0:T(128)S(1)} %broadcast_divide_fusion.11) | copy-start | bytes 1540
  123.1 63.6 %copy-start.52 = (f32[864]{0:T(1024)}, f32[864]{0:T(1024)S(1)}, u32[]{:S(2)}) copy-start(f32[864]{0:T(1024)S(1)} %fusion.100) | copy-start | bytes 10372
  123.7 63.0 %copy-start.76 = (f32[128]{0:T(128)}, f32[128]{0:T(128)S(1)}, u32[]{:S(2)}) copy-start(f32[128]{0:T(128)S(1)} %get-tuple-element.148) | copy-start | bytes 1540
  123.7 64.8 %copy-start.79 = (f32[128]{0:T(128)}, f32[128]{0:T(128)S(1)}, u32[]{:S(2)}) copy-start(f32[128]{0:T(128)S(1)} %get-tuple-element.149) | copy-start | bytes 1540
  123.7 162.6 %copy-start.77 = (f32[128]{0:T(128)}, f32[128]{0:T(128)S(1)}, u32[]{:S(2)}) copy-start(f32[128]{0:T(128)S(1)} %get-tuple-element.147) | copy-start | bytes 1540
  124.8 61.9 %reduce-scatter.5.cloned.1.call-start = ((), (), s32[]{:S(2)}) async-start(), calls=%async_computation.5 | async-start | bytes 2211840 | tf_op jit(solution)/shard_map/reduce_scatter | solution.py:122
  157.2 88.9 %all-gather.7.cloned.1.call-start = ((), (), s32[]{:S(2)}) async-start(), calls=%async_computation.6 | async-start | bytes 2211840 | tf_op jit(solution)/shard_map/all_gather | solution.py:120
  157.2 5.4 collective-permute-start.1
  188.8 5.5 collective-permute-start
  222.9 63.4 %copy-start.54 = (f32[864]{0:T(1024)}, f32[864]{0:T(1024)S(1)}, u32[]{:S(2)}) copy-start(f32[864]{0:T(1024)S(1)} %fusion.102) | copy-start | bytes 10372
  224.0 62.3 %reduce-scatter.7.cloned.1.call-start = ((), (), s32[]{:S(2)}) async-start(), calls=%async_computation.7 | async-start | bytes 2211840 | tf_op jit(solution)/shard_map/reduce_scatter | solution.py:122
  256.8 204.3 %all-gather.9.cloned.1.call-start = ((), (), s32[]{:S(2)}) async-start(), calls=%async_computation.8 | async-start | bytes 2211840 | tf_op jit(solution)/shard_map/all_gather | solution.py:128
  293.4 7.0 collective-permute-start.2
  293.5 140.0 %copy-start.50 = (f32[864]{0:T(1024)S(1)}, f32[864]{0:T(1024)}, u32[]{:S(2)}) copy-start(f32[864]{0:T(1024)} %copy-done.49) | copy-start | bytes 10372
  293.5 140.0 %copy-start.60 = (f32[864]{0:T(1024)S(1)}, f32[864]{0:T(1024)}, u32[]{:S(2)}) copy-start(f32[864]{0:T(1024)} %copy-done.59) | copy-start | bytes 10372
  293.5 142.2 %copy-start.70 = (f32[864]{0:T(1024)S(1)}, f32[864]{0:T(1024)}, u32[]{:S(2)}) copy-start(f32[864]{0:T(1024)} %copy-done.69) | copy-start | bytes 10372
  426.0 4.2 collective-permute-start.3
  433.5 67.3 %copy-start.55 = (f32[864]{0:T(1024)S(1)}, f32[864]{0:T(1024)}, u32[]{:S(2)}) copy-start(f32[864]{0:T(1024)} %copy-done.54) | copy-start | bytes 10372
  433.5 67.3 %copy-start.78 = (f32[128]{0:T(128)S(1)}, f32[128]{0:T(128)}, u32[]{:S(2)}) copy-start(f32[128]{0:T(128)} %copy-done.77) | copy-start | bytes 1540
  433.5 69.4 %copy-start.68 = (f32[864]{0:T(1024)S(1)}, f32[864]{0:T(1024)}, u32[]{:S(2)}) copy-start(f32[864]{0:T(1024)} %copy-done.67) | copy-start | bytes 10372
  439.0 61.8 %copy-start.18 = (f32[864,128]{1,0:T(8,128)S(1)}, f32[864,128]{1,0:T(8,128)}, u32[]{:S(2)}) copy-start(f32[864,128]{1,0:T(8,128)} %get-tuple-element.77) | copy-start | bytes 1327108
  439.1 65.8 %copy-start.40 = (f32[6,8,144]{2,1,0:T(8,128)S(1)}, f32[6,8,144]{2,1,0:T(8,128)}, u32[]{:S(2)}) copy-start(f32[6,8,144]{2,1,0:T(8,128)} %copy-done.39) | copy-start | bytes 82948
  439.1 61.7 %reduce-scatter.9.cloned.1.call-start = ((), (), s32[]{:S(2)}) async-start(), calls=%async_computation.9 | async-start | bytes 2211840 | tf_op jit(solution)/shard_map/reduce_scatter | solution.py:135
  471.2 120.6 %all-gather.11.cloned.1.call-start = ((), (), s32[]{:S(2)}) async-start(), calls=%async_computation.10 | async-start | bytes 2211840 | tf_op jit(solution)/shard_map/all_gather | solution.py:128
  561.4 7.0 collective-permute-start.4
  573.6 72.1 %reduce-scatter.11.cloned.1.call-start = ((), (), s32[]{:S(2)}) async-start(), calls=%async_computation.11 | async-start | bytes 2211840 | tf_op jit(solution)/shard_map/reduce_scatter | solution.py:135
  602.1 279.5 %all-reduce.14.cloned.1.call-start = ((), (), s32[]{:S(2)}) async-start(), calls=%async_computation.12 | async-start | bytes 1179648 | tf_op jit(solution)/shard_map/psum | solution.py:277
  707.9 48.7 %copy-start.95 = (f32[128]{0:T(128)S(1)}, f32[128]{0:T(128)}, u32[]{:S(2)}) copy-start(f32[128]{0:T(128)} %copy-done.94) | copy-start | bytes 1540
  707.9 49.3 %copy-start.93 = (f32[128]{0:T(128)S(1)}, f32[128]{0:T(128)}, u32[]{:S(2)}) copy-start(f32[128]{0:T(128)} %copy-done.92) | copy-start | bytes 1540
  751.8 204.0 %all-reduce.16.cloned.1.call-start = ((), (), s32[]{:S(2)}) async-start(), calls=%async_computation.13 | async-start | bytes 262144 | tf_op jit(solution)/shard_map/psum | solution.py:282
  (97 other events, 1481.7 us)
Sparse Core Ops, SparseCore 0:
  124.9 21.3 all-gather.4
  157.3 29.3 reduce-scatter.4
  224.1 21.9 all-gather.6
  256.9 29.3 reduce-scatter.6
  439.2 21.8 all-gather.8
  471.4 29.3 reduce-scatter.8
  573.8 18.0 all-gather.10
  602.2 29.3 reduce-scatter.10
  751.9 129.6 all-reduce.13
  885.8 69.9 all-reduce.15
where the time goes:
time: 982 us; the launch traced here: 969 us
  waiting for transfers between devices  373 us (38%)
  blocking collectives  260 us (26%)
  matrix products  177 us (18%)
  other arithmetic  73 us (7%)
  local copies, waits for them, and re-layouts  58.8 us (6%)
  between operations  16.1 us (2%)
  starting transfers between devices  12.1 us (1%)
    psum x1, waiting for transfers between devices, on_device(): lax.psum((local_w_vfe, stacked[0], stacked[1], stacked[5], local_ln_gain,...  124 us
    psum x2, blocking collectives, norm_stats(): lax.psum(jnp.sum(live_rows * (values - center) ** 2, axis=0), ('win', 'ff...  80.6 us
    psum x2, blocking collectives, norm_stats(): lax.psum((jnp.sum(live_rows * values, axis=0), jnp.sum(live_rows)), ('win...  79.9 us
    psum x2, blocking collectives, norm_back(): lax.psum((jnp.sum(grad_output * normed_hat, axis=0), jnp.sum(grad_output,...  77.1 us
    psum x1, waiting for transfers between devices, on_device(): lax.psum((shard_in, shard_bias, shard_back), 'win')  72.7 us
    dot_general x6, matrix products, window_core(): jnp.einsum('whqk,wkhe->wqhe', weights, value_rows, precision=lax.Precisio...  51.7 us
    reduce_scatter x2, waiting for transfers between devices, ffn_forward(): lax.psum_scatter(matmul(hidden, back_one), 'ffn', scatter_dimension=0, ti...  49.8 us
    dot_general x6, matrix products, window_core(): jnp.einsum('wqhe,wkhe->whqk', queries, key_rows, precision=lax.Precision....  44.7 us
  transfers between devices with their start and end apart: 15, of which 14 were waited for; matrix products, arithmetic and copies ran while one was open for 4% of the time, Pallas kernels for 0%

commit v1 on v0

v1 whole, which is shorter than its diff:
```python
import functools

import jax
import jax.numpy as jnp
from jax import lax
from jax.experimental import pallas as pl
from jax.experimental.pallas import tpu as pltpu
from jax.sharding import PartitionSpec as P

HEADS = 8
CELLS = 144
HALF = CELLS // 2
WIDTH = 128
EPS_NORM = 1e-05
NEG_FILL = -1000000000.0
AXES = ("win", "ffn")
STEP = 2 * CELLS
TILE_ROWS = WIDTH // HEADS
TILES = CELLS // TILE_ROWS
CHUNKS = ((0, 2), (2, 4), (4, 6), (6, 8), (8, 9))
F32 = jnp.float32
BF16 = jnp.bfloat16
VMEM_LIMIT = 56 * 1024 * 1024


def shape(*dims, dtype=F32):
    return jax.ShapeDtypeStruct(dims, dtype)


def whole(*dims):
    return pl.BlockSpec(dims, lambda i: (0,) * len(dims))


def rows_of(*dims):
    return pl.BlockSpec(dims, lambda i: (i,) + (0,) * (len(dims) - 1))


def share_of(rows, devices):
    return -(-rows // devices)


def halves(values):
    high = values.astype(BF16)
    return high, (values - high.astype(F32)).astype(BF16)


def nn(former, latter):
    return lax.dot_general(former, latter, (((1,), (0,)), ((), ())), preferred_element_type=F32)


def nt(former, latter):
    return lax.dot_general(former, latter, (((1,), (1,)), ((), ())), preferred_element_type=F32)


def tn(former, latter):
    return lax.dot_general(former, latter, (((0,), (0,)), ((), ())), preferred_element_type=F32)


def product(kind, former, latter):
    return kind(former[0], latter[0]) + (kind(former[0], latter[1]) + kind(former[1], latter[0]))


def gelu_parts(values):
    below = 0.5 * (1.0 + lax.erf(values * 0.7071067811865476))
    density = 0.3989422804014327 * jnp.exp(-0.5 * values * values)
    return values * below, below + values * density


def normed_rows(values):
    center = jnp.mean(values, axis=-1, keepdims=True)
    moved = values - center
    rate = lax.rsqrt(jnp.mean(moved * moved, axis=-1, keepdims=True) + EPS_NORM)
    return moved * rate, rate


def normed_back(grad, hat, rate, gain):
    scaled = grad * gain
    first = jnp.mean(scaled, axis=-1, keepdims=True)
    second = jnp.mean(scaled * hat, axis=-1, keepdims=True)
    return rate * (scaled - first - hat * second)


def column_sum(values):
    return jnp.sum(values, axis=0, keepdims=True)


def head_mask():
    dims = (HEADS, TILE_ROWS, WIDTH)
    lane_head = lax.broadcasted_iota(jnp.int32, dims, 2) // TILE_ROWS
    return (lane_head == lax.broadcasted_iota(jnp.int32, dims, 0)).astype(F32)


def per_head(rows, mask):
    count = rows.shape[0] // TILE_ROWS
    return (rows.reshape(count, 1, TILE_ROWS, WIDTH) * mask[None]).reshape(count * WIDTH, WIDTH)


def from_heads(table, mask):
    parts = []
    for at in range(0, table.shape[1], WIDTH):
        turned = table[:, at : at + WIDTH].T.reshape(HEADS, TILE_ROWS, WIDTH)
        parts.append(jnp.sum(turned * mask, axis=0))
    return parts


def window_mix(query, key, value, live, mask, mask_low, keep_high, keep_low):
    query_high, query_low = halves(query)
    key_high, key_low = halves(key)
    key_stack = jnp.concatenate([key_high, key_low, key_high], axis=1)
    turned = halves(value.T)
    mixed = []
    for first, last in CHUNKS:
        rows = slice(first * TILE_ROWS, last * TILE_ROWS)
        lanes = slice(first * WIDTH, last * WIDTH)
        high = per_head(query_high[rows], mask_low)
        low = per_head(query_low[rows], mask_low)
        scores = nt(key_stack, jnp.concatenate([high, high, low], axis=1))
        scores = jnp.where(live > 0, scores, NEG_FILL)
        weights = jnp.exp(scores - jnp.max(scores, axis=0, keepdims=True))
        weights = weights * (1.0 / column_sum(weights))
        weights = halves(weights)
        keep_high[:, lanes] = weights[0]
        keep_low[:, lanes] = weights[1]
        mixed += from_heads(product(nn, turned, weights), mask)
    return jnp.concatenate(mixed, axis=0)


def window_back(query, key, value, grad_mixed, live, mask, mask_low, kept_high, kept_low):
    query_halves = halves(query)
    grad_halves = halves(grad_mixed)
    value_high, value_low = halves(value)
    value_stack = jnp.concatenate([value_high, value_low, value_high], axis=1)
    turned = halves(key.T)
    grad_key = jnp.zeros((CELLS, 2 * WIDTH), F32)
    grad_value = jnp.zeros((CELLS, 2 * WIDTH), F32)
    key_rest = jnp.zeros((CELLS, WIDTH), F32)
    value_rest = jnp.zeros((CELLS, WIDTH), F32)
    grad_query = []
    for first, last in CHUNKS:
        rows = slice(first * TILE_ROWS, last * TILE_ROWS)
        lanes = slice(first * WIDTH, last * WIDTH)
        query_high, query_low = (per_head(part[rows], mask_low) for part in query_halves)
        grad_high, grad_low = (per_head(part[rows], mask_low) for part in grad_halves)
        grad_weights = nt(value_stack, jnp.concatenate([grad_high, grad_high, grad_low], axis=1))
        high, low = kept_high[:, lanes], kept_low[:, lanes]
        weights = high.astype(F32) + low.astype(F32)
        grad_scores = weights * grad_weights
        grad_scores = live * (grad_scores - weights * column_sum(grad_scores))
        scores_high, scores_low = halves(grad_scores)
        grad_value += nn(high, jnp.concatenate([grad_high, grad_low], axis=1))
        value_rest += nn(low, grad_high)
        grad_key += nn(scores_high, jnp.concatenate([query_high, query_low], axis=1))
        key_rest += nn(scores_low, query_high)
        grad_query += from_heads(product(nn, turned, (scores_high, scores_low)), mask)
    return (
        0.25 * jnp.concatenate(grad_query, axis=0),
        grad_key[:, :WIDTH] + (grad_key[:, WIDTH:] + key_rest),
        grad_value[:, :WIDTH] + (grad_value[:, WIDTH:] + value_rest),
    )


def unpack_weights(packed, one, up_high, up_low, down_high, down_low, bias):
    ffns = packed.shape[0]
    units = bias.shape[1] // ffns
    for at in range(ffns):
        rows = slice(at * units, (at + 1) * units)
        high, low = halves(packed[at, one * units : (one + 1) * units])
        up_high[rows], up_low[rows] = high, low
        high, low = halves(packed[at, (2 + one) * units : (3 + one) * units])
        down_high[rows], down_low[rows] = high, low
    bias[...] = jnp.concatenate(
        [packed[at, 4 * units + one : 4 * units + one + 1, :units] for at in range(ffns)], axis=1
    )


def layer_rows(one, values, live, weights, saved):
    qkv_high, qkv_low, out_high, out_low, up, down, bias, back_bias, gains, offsets = weights
    packed_keep, high_keep, low_keep, mixed_keep, hat_one, rate_one, hidden_keep, slope, hat_two, rate_two = saved
    mask = head_mask()
    mask_low = mask.astype(BF16)
    qkv = product(nn, halves(values), (qkv_high[one], qkv_low[one]))
    query = 0.25 * qkv[:, :WIDTH]
    packed_keep[:, :WIDTH] = query
    packed_keep[:, WIDTH:] = qkv[:, WIDTH:]
    for at in range(STEP // CELLS):
        rows = slice(at * CELLS, (at + 1) * CELLS)
        mixed_keep[rows] = window_mix(
            query[rows],
            qkv[rows, WIDTH : 2 * WIDTH],
            qkv[rows, 2 * WIDTH :],
            live[rows],
            mask,
            mask_low,
            high_keep.at[at],
            low_keep.at[at],
        )
    mixed = mixed_keep[...]
    hat, rate = normed_rows(
        values + product(nn, halves(mixed), (out_high[one], out_low[one]))
    )
    hat_one[...] = hat
    rate_one[...] = jnp.broadcast_to(rate, hat.shape)
    first = hat * gains[2 * one : 2 * one + 1] + offsets[2 * one : 2 * one + 1]
    hidden, steep = gelu_parts(product(nt, halves(first), up) + bias)
    hidden_keep[...] = hidden
    slope[...] = steep
    summed = first + product(nn, halves(hidden), down) + back_bias[one : one + 1]
    hat, rate = normed_rows(summed)
    hat_two[...] = hat
    rate_two[...] = jnp.broadcast_to(rate, hat.shape)
    return hat * gains[2 * one + 1 : 2 * one + 2] + offsets[2 * one + 1 : 2 * one + 2]


def ffn_rows_back(one, grad, saved, weights, sums):
    mixed_keep, hat_one, rate_one, hidden_keep, slope, hat_two, rate_two = saved
    out, up, down, gains, offsets = weights
    small, sum_out, sum_up, sum_down = sums
    hat = hat_two[...]
    grad_summed = normed_back(grad, hat, rate_two[...], gains[2 * one + 1 : 2 * one + 2])
    small[3:4] += column_sum(grad * hat)
    small[4:5] += column_sum(grad)
    small[0:1] += column_sum(grad_summed)
    summed_halves = halves(grad_summed)
    grad_pre = product(nt, summed_halves, down) * slope[...]
    pre_halves = halves(grad_pre)
    hidden_halves = halves(hidden_keep[...])
    sum_down[...] += product(tn, hidden_halves, summed_halves)
    hat = hat_one[...]
    first = hat * gains[2 * one : 2 * one + 1] + offsets[2 * one : 2 * one + 1]
    sum_up[...] += product(tn, pre_halves, halves(first))
    bias_sum = column_sum(grad_pre)
    for at in range(bias_sum.shape[1] // WIDTH):
        small[5 + at : 6 + at] += bias_sum[:, at * WIDTH : (at + 1) * WIDTH]
    grad_first = grad_summed + product(nn, pre_halves, up)
    small[1:2] += column_sum(grad_first * hat)
    small[2:3] += column_sum(grad_first)
    grad_joined = normed_back(grad_first, hat, rate_one[...], gains[2 * one : 2 * one + 1])
    joined_halves = halves(grad_joined)
    sum_out[...] += product(tn, halves(mixed_keep[...]), joined_halves)
    return grad_joined, product(nt, joined_halves, out)


def attention_rows_back(one, values, live, grad_joined, grad_mixed, saved, qkv_weights, sum_qkv):
    packed_keep, high_keep, low_keep = saved
    mask = head_mask()
    mask_low = mask.astype(BF16)
    parts = []
    for at in range(STEP // CELLS):
        rows = slice(at * CELLS, (at + 1) * CELLS)
        parts.append(
            window_back(
                packed_keep[rows, :WIDTH],
                packed_keep[rows, WIDTH : 2 * WIDTH],
                packed_keep[rows, 2 * WIDTH :],
                grad_mixed[rows],
                live[rows],
                mask,
                mask_low,
                high_keep.at[at],
                low_keep.at[at],
            )
        )
    grad_packed = halves(
        jnp.concatenate([jnp.concatenate(part, axis=1) for part in parts], axis=0)
    )
    sum_qkv[...] += product(tn, halves(values), grad_packed)
    return grad_joined + product(nt, grad_packed, (qkv_weights[0][one], qkv_weights[1][one]))


def share_rows(target, at, values, devices):
    count = values.shape[0]
    share = share_of(count, devices)
    for device in range(devices):
        begin = device * share
        if begin < count:
            held = min(share, count - begin)
            target[device, at : at + held] = values[begin : begin + held]
    return at + share


def share_units(target, at, sum_up, sum_down, wins, ffns):
    units = sum_up.shape[0] // ffns
    part = 2 * units // wins
    for f in range(ffns):
        rows = slice(f * units, (f + 1) * units)
        joined = jnp.concatenate([sum_up[rows], sum_down[rows]], axis=0)
        for w in range(wins):
            target[w * ffns + f, at : at + part] = joined[w * part : (w + 1) * part]
    return at + part


def joined_rows(table, at, count):
    devices = table.shape[0]
    share = share_of(count, devices)
    if share % 8 == 0 and share * devices == count:
        return table[:, at : at + share].reshape(count, WIDTH)
    pieces = []
    for device in range(devices):
        begin = device * share
        if begin < count:
            pieces.append(table[device, at : at + min(share, count - begin)])
    return jnp.concatenate(pieces, axis=0)


def vfe_kernel(
    feats_ref, weight_ref, occupied_ref, up_ref, down_ref, bias_ref, lifted_ref, live_ref, sent_ref, packed_ref
):
    devices = sent_ref.shape[0]
    units = up_ref.shape[2]
    feats = feats_ref[...]
    row_count = feats.shape[0]
    feats_halves = halves(feats)
    lifted = product(nn, feats_halves, halves(weight_ref[...]))
    lifted_ref[...] = lifted
    live = jnp.broadcast_to(occupied_ref[...].astype(F32), (8, row_count)).T[:, :1]
    live_ref[...] = live
    count = jnp.sum(live, axis=0, keepdims=True)
    total = column_sum(live * lifted)
    moved = live * (lifted - total / jnp.maximum(count, 1.0))
    sent_ref[...] = jnp.zeros(sent_ref.shape, F32)
    stats = jnp.concatenate(
        [
            jnp.broadcast_to(count, (1, WIDTH)),
            total,
            column_sum(moved * moved),
            column_sum(live * feats),
        ],
        axis=0,
    )
    sent_ref[:, 0:4] = jnp.broadcast_to(stats[None], (devices, 4, WIDTH))
    share_rows(sent_ref, 4, product(tn, feats_halves, halves(moved)), devices)
    turned = (up_ref[0].T, up_ref[1].T)
    for to in range(packed_ref.shape[0]):
        for one in range(2):
            packed_ref[to, one * units : (one + 1) * units] = turned[one]
            packed_ref[to, (2 + one) * units : (3 + one) * units] = down_ref[one]
        packed_ref[to, 4 * units :] = jnp.zeros((8, WIDTH), F32)
        packed_ref[to, 4 * units : 4 * units + 2, :units] = bias_ref[...]


def maps_kernel(source_ref, qkv_ref, out_ref, gather_ref, scatter_ref, qkv_high, qkv_low, out_high, out_low):
    row_count = source_ref.shape[1]
    held = gather_ref.shape[1]
    devices = lax.axis_size(AXES)
    places = source_ref[...] - lax.axis_index(AXES) * row_count
    places = jnp.where(places < 0, places + row_count * devices, places)
    column = jnp.broadcast_to(places.astype(F32), (8, row_count)).T[:, :1].astype(jnp.int32)
    for at in range(row_count // STEP):
        rows = slice(at * STEP, (at + 1) * STEP)
        lanes = lax.broadcasted_iota(jnp.int32, (STEP, held), 1)
        gather_ref[rows] = (lanes == column[rows]).astype(F32).astype(BF16)
        down = lax.broadcasted_iota(jnp.int32, (held, STEP), 0)
        scatter_ref[at] = (down == places[:, rows]).astype(F32).astype(BF16)
    qkv_high[...], qkv_low[...] = halves(qkv_ref[...])
    out_high[...], out_low[...] = halves(out_ref[...])


def vfe_stats(seen_ref, gain_ref, shift_ref, stats_ref, product_ref):
    counts, totals, squares, lives = (seen_ref[:, at] for at in range(4))
    count = column_sum(counts)
    center = column_sum(totals) / count
    moves = totals / jnp.maximum(counts, 1.0) - center
    rate = lax.rsqrt(column_sum(squares + counts * moves * moves) / count + EPS_NORM)
    stats_ref[...] = jnp.zeros(stats_ref.shape, F32)
    stats_ref[0:1] = count
    stats_ref[1:2] = center
    stats_ref[2:3] = rate
    stats_ref[3:4] = column_sum(lives)
    devices = seen_ref.shape[0]
    share = share_of(WIDTH, devices)
    mine = lax.axis_index(AXES) * share
    lanes = lax.broadcasted_iota(jnp.int32, lives.shape, 1)
    product_ref[...] = jnp.zeros(product_ref.shape, F32)
    for at in range(share):
        picked = jnp.sum(jnp.where(lanes == mine + at, lives, 0.0), axis=1, keepdims=True)
        product_ref[at : at + 1] = rate * column_sum(seen_ref[:, 4 + at] + picked * moves)


def first_kernel(
    lifted_ref,
    live_ref,
    cotangent_ref,
    seen_ref,
    bn_gain,
    bn_shift,
    qkv_high,
    qkv_low,
    out_high,
    out_low,
    packed,
    back_bias,
    gains,
    offsets,
    result,
    edge,
    stats,
    hat_product,
    vfe_hat,
    vfe_slope,
    carried,
    packed_keep,
    high_keep,
    low_keep,
    mixed_keep,
    hat_one,
    rate_one,
    hidden_keep,
    slope,
    hat_two,
    rate_two,
    up_high,
    up_low,
    down_high,
    down_low,
    bias,
):
    at = pl.program_id(0)

    @pl.when(at == 0)
    def _():
        unpack_weights(packed, 0, up_high, up_low, down_high, down_low, bias)
        vfe_stats(seen_ref, bn_gain, bn_shift, stats, hat_product)

    hat = (lifted_ref[...] - stats[1:2]) * stats[2:3]
    values, steep = gelu_parts(hat * bn_gain[0:1] + bn_shift[0:1])
    vfe_hat[...] = hat
    vfe_slope[...] = steep
    carried[...] = values
    live = live_ref[...]
    rows = layer_rows(
        0,
        values,
        live,
        (
            qkv_high,
            qkv_low,
            out_high,
            out_low,
            (up_high[...], up_low[...]),
            (down_high[...], down_low[...]),
            bias[...],
            back_bias,
            gains,
            offsets,
        ),
        (packed_keep, high_keep, low_keep, mixed_keep, hat_one, rate_one, hidden_keep, slope, hat_two, rate_two),
    )
    result[...] = rows

    @pl.when(at == 0)
    def _():
        edge[:, :WIDTH] = rows[:HALF]
        edge[:, WIDTH : 2 * WIDTH] = cotangent_ref[:HALF]
        edge[:, 2 * WIDTH :] = jnp.broadcast_to(live[:HALF], (HALF, WIDTH))


def second_kernel(
    first_ref,
    cotangent_ref,
    live_ref,
    edge,
    gather_ref,
    qkv_high,
    qkv_low,
    out_high,
    out_low,
    packed,
    back_bias,
    gains,
    offsets,
    result,
    sent,
    live_keep,
    cotangent_keep,
    carried,
    packed_keep,
    high_keep,
    low_keep,
    mixed_keep,
    hat_one,
    rate_one,
    hidden_keep,
    slope,
    hat_two,
    rate_two,
    up_high,
    up_low,
    down_high,
    down_low,
    bias,
    table,
    sums,
):
    at = pl.program_id(0)
    row_count = first_ref.shape[0]

    @pl.when(at == 0)
    def _():
        unpack_weights(packed, 1, up_high, up_low, down_high, down_low, bias)
        high, low = halves(first_ref[...])
        table[:row_count, :WIDTH] = high
        table[:row_count, WIDTH : 2 * WIDTH] = low
        high, low = halves(cotangent_ref[...])
        table[:row_count, 2 * WIDTH : 3 * WIDTH] = high
        table[:row_count, 3 * WIDTH : 4 * WIDTH] = low
        table[:row_count, 4 * WIDTH :] = jnp.broadcast_to(live_ref[...], (row_count, WIDTH)).astype(BF16)
        spare = table.shape[0] - row_count
        tail = jnp.concatenate([edge[...], jnp.zeros((spare - HALF, 3 * WIDTH), F32)], axis=0)
        high, low = halves(tail)
        table[row_count:, :WIDTH] = high[:, :WIDTH]
        table[row_count:, WIDTH : 2 * WIDTH] = low[:, :WIDTH]
        table[row_count:, 2 * WIDTH : 3 * WIDTH] = high[:, WIDTH : 2 * WIDTH]
        table[row_count:, 3 * WIDTH : 4 * WIDTH] = low[:, WIDTH : 2 * WIDTH]
        table[row_count:, 4 * WIDTH :] = high[:, 2 * WIDTH :]
        sums[...] = jnp.zeros(sums.shape, F32)

    gathered = nn(gather_ref[...], table[...])
    values = gathered[:, :WIDTH] + gathered[:, WIDTH : 2 * WIDTH]
    live = gathered[:, 4 * WIDTH :]
    grad = live * (gathered[:, 2 * WIDTH : 3 * WIDTH] + gathered[:, 3 * WIDTH : 4 * WIDTH])
    carried[...] = values
    cotangent_keep[...] = grad
    live_keep[...] = live[:, :1]
    rows = layer_rows(
        1,
        values,
        live[:, :1],
        (
            qkv_high,
            qkv_low,
            out_high,
            out_low,
            (up_high[...], up_low[...]),
            (down_high[...], down_low[...]),
            bias[...],
            back_bias,
            gains,
            offsets,
        ),
        (packed_keep, high_keep, low_keep, mixed_keep, hat_one, rate_one, hidden_keep, slope, hat_two, rate_two),
    )
    result[...] = rows
    count = column_sum(live)

    @pl.when(at == 0)
    def _():
        sums[5:6] = column_sum(live * rows) / jnp.maximum(count, 1.0)

    moved = rows - sums[5:6]
    sums[0:1] += count
    sums[1:2] += column_sum(live * moved)
    sums[2:3] += column_sum(live * moved * moved)
    sums[3:4] += column_sum(grad)
    sums[4:5] += column_sum(grad * moved)

    @pl.when(at == pl.num_programs(0) - 1)
    def _():
        count = sums[0:1]
        move = sums[1:2] / jnp.maximum(count, 1.0)
        stats = jnp.concatenate(
            [
                count,
                sums[5:6] + move,
                sums[2:3] - count * move * move,
                sums[3:4],
                sums[4:5] - move * sums[3:4],
                jnp.zeros((3, WIDTH), F32),
            ],
            axis=0,
        )
        sent[...] = jnp.broadcast_to(stats[None], sent.shape)


def second_back_kernel(
    result,
    seen_ref,
    bn_gain,
    bn_shift,
    scatter_ref,
    qkv_high,
    qkv_low,
    out_high,
    out_low,
    packed,
    gains,
    offsets,
    live_keep,
    cotangent_keep,
    carried,
    packed_keep,
    high_keep,
    low_keep,
    mixed_keep,
    hat_one,
    rate_one,
    hidden_keep,
    slope,
    hat_two,
    rate_two,
    shared,
    edge,
    grad_rows,
    out_rows,
    neck,
    up_high,
    up_low,
    down_high,
    down_low,
    bias,
    stats,
    small,
    sum_qkv,
    sum_out,
    sum_up,
    sum_down,
    placed,
    *,
    wins,
    ffns,
):
    at = pl.program_id(0)
    row_count = grad_rows.shape[0]

    @pl.when(at == 0)
    def _():
        unpack_weights(packed, 1, up_high, up_low, down_high, down_low, bias)
        counts, means, squares, grads, products = (seen_ref[:, row] for row in range(5))
        count = column_sum(counts)
        center = column_sum(counts * means) / count
        moves = means - center
        rate = lax.rsqrt(column_sum(squares + counts * moves * moves) / count + EPS_NORM)
        stats[0:1] = count
        stats[1:2] = center
        stats[2:3] = rate
        stats[3:4] = rate * column_sum(products + moves * grads)
        stats[4:5] = column_sum(grads)
        neck[...] = jnp.zeros(neck.shape, F32)
        neck[0:2] = stats[3:5]
        for held in (small, sum_qkv, sum_out, sum_up, sum_down, placed):
            held[...] = jnp.zeros(held.shape, F32)

    live = live_keep[...]
    rate = stats[2:3]
    hat = (result[...] - stats[1:2]) * rate
    neck_rows = live * (hat * bn_gain[1:2] + bn_shift[1:2])
    grad = rate * bn_gain[1:2] * (
        cotangent_keep[...] - live * (hat * stats[3:4] + stats[4:5]) / stats[0:1]
    )
    grad_joined, grad_mixed = ffn_rows_back(
        1,
        grad,
        (mixed_keep, hat_one, rate_one, hidden_keep, slope, hat_two, rate_two),
        (
            (out_high[1], out_low[1]),
            (up_high[...], up_low[...]),
            (down_high[...], down_low[...]),
            gains,
            offsets,
        ),
        (small, sum_out, sum_up, sum_down),
    )
    grad_values = attention_rows_back(
        1,
        carried[...],
        live,
        grad_joined,
        grad_mixed,
        (packed_keep, high_keep, low_keep),
        (qkv_high, qkv_low),
        sum_qkv,
    )
    pieces = halves(grad_values) + halves(neck_rows)
    moved = nn(scatter_ref[0], jnp.concatenate(pieces, axis=1))
    placed[:, :WIDTH] += moved[:, :WIDTH] + moved[:, WIDTH : 2 * WIDTH]
    placed[:, WIDTH:] += moved[:, 2 * WIDTH : 3 * WIDTH] + moved[:, 3 * WIDTH :]

    @pl.when(at == pl.num_programs(0) - 1)
    def _():
        grad_rows[...] = placed[:row_count, :WIDTH]
        out_rows[...] = placed[:row_count, WIDTH:]
        edge[...] = placed[row_count : row_count + HALF]
        devices = wins * ffns
        shared[...] = jnp.zeros(shared.shape, F32)
        row = share_units(shared, 0, sum_up, sum_down, wins, ffns)
        for block in range(3):
            row = share_rows(shared, row, sum_qkv[:, block * WIDTH : (block + 1) * WIDTH], devices)
        row = share_rows(shared, row, sum_out, devices)
        share_rows(shared, row, small, devices)


def first_ffn_back_kernel(
    grad_rows,
    edge,
    out_rows,
    out_high,
    out_low,
    packed,
    gains,
    offsets,
    mixed_keep,
    hat_one,
    rate_one,
    hidden_keep,
    slope,
    hat_two,
    rate_two,
    grad_joined,
    grad_mixed,
    pillars,
    shared,
    up_high,
    up_low,
    down_high,
    down_low,
    bias,
    small,
    sum_out,
    sum_up,
    sum_down,
    grad_step,
    *,
    wins,
    ffns,
):
    at = pl.program_id(0)

    @pl.when(at == 0)
    def _():
        unpack_weights(packed, 0, up_high, up_low, down_high, down_low, bias)
        for held in (small, sum_out, sum_up, sum_down):
            held[...] = jnp.zeros(held.shape, F32)

    grad_step[...] = grad_rows[...]
    pillars[...] = out_rows[...]

    @pl.when(at == 0)
    def _():
        grad_step[:HALF] = edge[:, :WIDTH]
        pillars[:HALF] = edge[:, WIDTH:]

    joined, mixed = ffn_rows_back(
        0,
        grad_step[...],
        (mixed_keep, hat_one, rate_one, hidden_keep, slope, hat_two, rate_two),
        (
            (out_high[0], out_low[0]),
            (up_high[...], up_low[...]),
            (down_high[...], down_low[...]),
            gains,
            offsets,
        ),
        (small, sum_out, sum_up, sum_down),
    )
    grad_joined[...] = joined
    grad_mixed[...] = mixed

    @pl.when(at == pl.num_programs(0) - 1)
    def _():
        shared[...] = jnp.zeros(shared.shape, F32)
        row = share_units(shared, 0, sum_up, sum_down, wins, ffns)
        row = share_rows(shared, row, sum_out, wins * ffns)
        share_rows(shared, row, small, wins * ffns)


def first_attention_back_kernel(
    grad_joined,
    grad_mixed,
    feats_ref,
    live_ref,
    carried,
    vfe_hat,
    vfe_slope,
    qkv_high,
    qkv_low,
    packed_keep,
    high_keep,
    low_keep,
    grad_affine,
    shared,
    sent,
    sum_qkv,
    sum_feats,
    small,
):
    at = pl.program_id(0)

    @pl.when(at == 0)
    def _():
        for held in (small, sum_qkv, sum_feats):
            held[...] = jnp.zeros(held.shape, F32)

    grad = attention_rows_back(
        0,
        carried[...],
        live_ref[...],
        grad_joined[...],
        grad_mixed[...],
        (packed_keep, high_keep, low_keep),
        (qkv_high, qkv_low),
        sum_qkv,
    )
    grad = grad * vfe_slope[...]
    grad_affine[...] = grad
    small[0:1] += column_sum(grad * vfe_hat[...])
    small[1:2] += column_sum(grad)
    sum_feats[...] += product(tn, halves(feats_ref[...]), halves(grad))

    @pl.when(at == pl.num_programs(0) - 1)
    def _():
        devices = shared.shape[0]
        shared[...] = jnp.zeros(shared.shape, F32)
        row = 0
        for block in range(3):
            row = share_rows(shared, row, sum_qkv[:, block * WIDTH : (block + 1) * WIDTH], devices)
        share_rows(shared, row, sum_feats, devices)
        sent[...] = jnp.broadcast_to(small[...][None], sent.shape)


def relay_kernel(*refs, split, count, extra):
    arrived = refs[0]
    total = jnp.sum(arrived[...], axis=0)
    outs = refs[2:] if extra else refs[1:]
    if split:
        outs[1][...] = jnp.broadcast_to(total[:split][None], outs[1].shape)
    rows = total[split : split + count]
    if extra:
        rows = jnp.concatenate([rows, refs[1][:extra]], axis=0)
    room = outs[0].shape[1]
    if rows.shape[0] < room:
        rows = jnp.concatenate([rows, jnp.zeros((room - rows.shape[0], WIDTH), F32)], axis=0)
    outs[0][...] = jnp.broadcast_to(rows[:room][None], outs[0].shape)


def feats_back_kernel(grad_affine, vfe_hat, live_ref, stats, seen_ref, bn_gain, weight_ref, grad_feats, vfe_grads):
    sums = jnp.sum(seen_ref[...], axis=0)
    vfe_grads[...] = sums
    scale = stats[2:3] * bn_gain[0:1]
    grad = scale * (
        grad_affine[...]
        - live_ref[...] * (vfe_hat[...] * sums[0:1] + sums[1:2]) / stats[0:1]
    )
    grad_feats[...] = product(nt, halves(grad), halves(weight_ref[...]))


def last_kernel(
    late,
    middle,
    early,
    late_units,
    early_units,
    stats,
    vfe_grads,
    neck,
    bn_gain,
    grad_w_vfe,
    grad_bn_gain,
    grad_bn_shift,
    grad_w_qkv,
    grad_w_out,
    grad_w_in,
    grad_b_in,
    grad_w_back,
    grad_b_back,
    grad_ln_gain,
    grad_ln_shift,
    *,
    ffns,
):
    devices = late.shape[0]
    part = share_of(WIDTH, devices)
    units = grad_w_in.shape[2]
    wins = late_units.shape[0]
    piece = 2 * units // wins
    for block in range(3):
        lanes = slice(block * WIDTH, (block + 1) * WIDTH)
        grad_w_qkv[0, :, lanes] = joined_rows(late, block * part, WIDTH)
        grad_w_qkv[1, :, lanes] = joined_rows(early, block * part, WIDTH)
    feats_sum = joined_rows(late, 3 * part, WIDTH)
    grad_w_out[0] = joined_rows(middle, 0, WIDTH)
    grad_w_out[1] = joined_rows(early, 3 * part, WIDTH)
    small_rows = 8
    one = share_of(small_rows, devices)
    smalls = (
        joined_rows(middle, part, small_rows),
        joined_rows(early, 4 * part, small_rows),
    )
    hat_sum = joined_rows(early, 4 * part + one, WIDTH)
    mine = lax.rem(lax.axis_index(AXES), ffns)
    for layer in range(2):
        small = smalls[layer]
        grad_b_back[layer : layer + 1] = small[0:1]
        grad_ln_gain[2 * layer : 2 * layer + 1] = small[1:2]
        grad_ln_shift[2 * layer : 2 * layer + 1] = small[2:3]
        grad_ln_gain[2 * layer + 1 : 2 * layer + 2] = small[3:4]
        grad_ln_shift[2 * layer + 1 : 2 * layer + 2] = small[4:5]
        held = jnp.zeros((1, units), F32)
        for f in range(ffns):
            row, lane = divmod(f * units, WIDTH)
            held = jnp.where(mine == f, small[5 + row : 6 + row, lane : lane + units], held)
        grad_b_in[layer : layer + 1] = held
        table = (late_units, early_units)[layer]
        joined = joined_rows(table, 0, 2 * units)
        grad_w_in[layer] = joined[:units].T
        grad_w_back[layer] = joined[units:]
    gain, shift = vfe_grads[0:1], vfe_grads[1:2]
    grad_bn_gain[0:1] = gain
    grad_bn_gain[1:2] = neck[0:1]
    grad_bn_shift[0:1] = shift
    grad_bn_shift[1:2] = neck[1:2]
    live_sum = jnp.broadcast_to(stats[3:4], (8, WIDTH)).T[:, :1]
    grad_w_vfe[...] = stats[2:3] * bn_gain[0:1] * (
        feats_sum - (hat_sum * gain + live_sum * shift) / stats[0:1]
    )


def spread_rows(pieces, axes):
    return lax.all_to_all(pieces, axes, 0, 0)


def passed_along(rows, by):
    peers = lax.axis_size(AXES)
    return lax.ppermute(rows, AXES, [(i, (i + by) % peers) for i in range(peers)])


def params():
    return pltpu.CompilerParams(vmem_limit_bytes=VMEM_LIMIT)


def cost(flops, size):
    return pl.CostEstimate(flops=int(flops), bytes_accessed=int(size), transcendentals=0)


def on_device(
    pillar_feats,
    occupied,
    shifted_source_rows,
    w_vfe,
    bn_gain,
    bn_shift,
    query_key_value_weight,
    attention_output_weight,
    up_weight_matrix,
    up_bias_rows,
    down_weight_matrix,
    down_bias_rows,
    layernorm_gains,
    layernorm_offsets,
    cotangent,
):
    row_count = pillar_feats.shape[0]
    steps = row_count // STEP
    held = row_count + -(-HALF // 16) * 16
    wins, ffns = lax.axis_size("win"), lax.axis_size("ffn")
    devices = wins * ffns
    units = up_weight_matrix.shape[2]
    hidden = units * ffns
    part = share_of(WIDTH, devices)
    stats_rows = -(-(4 + part) // 8) * 8

    lifted, live, sent, packed = pl.pallas_call(
        vfe_kernel,
        out_shape=(
            shape(row_count, WIDTH),
            shape(row_count, 1),
            shape(devices, stats_rows, WIDTH),
            shape(ffns, 4 * units + 8, WIDTH),
        ),
        compiler_params=params(),
        name="vfe",
    )(
        pillar_feats,
        w_vfe,
        occupied.reshape(1, row_count),
        up_weight_matrix,
        down_weight_matrix,
        up_bias_rows,
    )
    seen = spread_rows(sent, AXES)
    packed = spread_rows(packed, "ffn")
    gather, scatter, qkv_high, qkv_low, out_high, out_low = pl.pallas_call(
        maps_kernel,
        out_shape=(
            shape(row_count, held, dtype=BF16),
            shape(steps, held, STEP, dtype=BF16),
            shape(2, WIDTH, 3 * WIDTH, dtype=BF16),
            shape(2, WIDTH, 3 * WIDTH, dtype=BF16),
            shape(2, WIDTH, WIDTH, dtype=BF16),
            shape(2, WIDTH, WIDTH, dtype=BF16),
        ),
        compiler_params=params(),
        cost_estimate=cost(1e8, 4e6),
        name="maps",
    )(shifted_source_rows.reshape(1, row_count), query_key_value_weight, attention_output_weight)

    rows_spec = rows_of(STEP, WIDTH)
    column_spec = rows_of(STEP, 1)
    qkv_specs = [whole(2, WIDTH, 3 * WIDTH)] * 2
    out_specs = [whole(2, WIDTH, WIDTH)] * 2
    packed_spec = whole(*packed.shape)
    norm_specs = [whole(4, WIDTH)] * 2
    pair_spec = whole(2, WIDTH)
    seen_spec = whole(devices, stats_rows, WIDTH)
    eight_spec = whole(8, WIDTH)
    unit_scratch = [pltpu.VMEM((hidden, WIDTH), BF16)] * 4 + [pltpu.VMEM((1, hidden), F32)]
    keep_specs = [
        rows_spec,
        rows_of(STEP, 3 * WIDTH),
        rows_of(STEP // CELLS, CELLS, HEADS * CELLS),
        rows_of(STEP // CELLS, CELLS, HEADS * CELLS),
        rows_spec,
        rows_spec,
        rows_spec,
        rows_of(STEP, hidden),
        rows_of(STEP, hidden),
        rows_spec,
        rows_spec,
    ]
    windows = row_count // CELLS
    row_shape = shape(row_count, WIDTH)
    keep_shapes = [
        row_shape,
        shape(row_count, 3 * WIDTH),
        shape(windows, CELLS, HEADS * CELLS, dtype=BF16),
        shape(windows, CELLS, HEADS * CELLS, dtype=BF16),
        row_shape,
        row_shape,
        row_shape,
        shape(row_count, hidden),
        shape(row_count, hidden),
        row_shape,
        row_shape,
    ]

    first_out, edge, stats, hat_product, vfe_hat, vfe_slope, *first_keep = pl.pallas_call(
        first_kernel,
        grid=(steps,),
        in_specs=[rows_spec, column_spec, rows_spec, seen_spec, pair_spec, pair_spec]
        + qkv_specs
        + out_specs
        + [packed_spec, pair_spec]
        + norm_specs,
        out_specs=[rows_spec, whole(HALF, 3 * WIDTH), eight_spec, eight_spec, rows_spec, rows_spec] + keep_specs,
        out_shape=[row_shape, shape(HALF, 3 * WIDTH), shape(8, WIDTH), shape(8, WIDTH), row_shape, row_shape]
        + keep_shapes,
        scratch_shapes=unit_scratch,
        compiler_params=params(),
        cost_estimate=cost(4e9, 12e6),
        name="first",
    )(
        lifted,
        live,
        cotangent,
        seen,
        bn_gain,
        bn_shift,
        qkv_high,
        qkv_low,
        out_high,
        out_low,
        packed,
        down_bias_rows,
        layernorm_gains,
        layernorm_offsets,
    )
    edge = passed_along(edge, -1)
    second_out, sent, live_keep, cotangent_keep, *second_keep = pl.pallas_call(
        second_kernel,
        grid=(steps,),
        in_specs=[
            whole(row_count, WIDTH),
            whole(row_count, WIDTH),
            whole(row_count, 1),
            whole(HALF, 3 * WIDTH),
            rows_of(STEP, held),
        ]
        + qkv_specs
        + out_specs
        + [packed_spec, pair_spec]
        + norm_specs,
        out_specs=[rows_spec, whole(devices, 8, WIDTH), column_spec, rows_spec] + keep_specs,
        out_shape=[row_shape, shape(devices, 8, WIDTH), shape(row_count, 1), row_shape] + keep_shapes,
        scratch_shapes=unit_scratch
        + [pltpu.VMEM((held, 5 * WIDTH), BF16), pltpu.VMEM((8, WIDTH), F32)],
        compiler_params=params(),
        cost_estimate=cost(4e9, 12e6),
        name="second",
    )(
        first_out,
        cotangent,
        live,
        edge,
        gather,
        qkv_high,
        qkv_low,
        out_high,
        out_low,
        packed,
        down_bias_rows,
        layernorm_gains,
        layernorm_offsets,
    )
    seen = spread_rows(sent, AXES)
    piece = 2 * units // wins
    early_rows = -(-(piece + 4 * part + share_of(8, devices)) // 8) * 8
    sum_scratch = [
        pltpu.VMEM((8, WIDTH), F32),
        pltpu.VMEM((WIDTH, 3 * WIDTH), F32),
        pltpu.VMEM((WIDTH, WIDTH), F32),
        pltpu.VMEM((hidden, WIDTH), F32),
        pltpu.VMEM((hidden, WIDTH), F32),
    ]
    shared, edge, grad_rows, out_rows, neck = pl.pallas_call(
        functools.partial(second_back_kernel, wins=wins, ffns=ffns),
        grid=(steps,),
        in_specs=[rows_spec, whole(devices, 8, WIDTH), pair_spec, pair_spec, rows_of(1, held, STEP)]
        + qkv_specs
        + out_specs
        + [packed_spec]
        + norm_specs
        + [column_spec, rows_spec]
        + keep_specs,
        out_specs=[
            whole(devices, early_rows, WIDTH),
            whole(HALF, 2 * WIDTH),
            whole(row_count, WIDTH),
            whole(row_count, WIDTH),
            eight_spec,
        ],
        out_shape=[
            shape(devices, early_rows, WIDTH),
            shape(HALF, 2 * WIDTH),
            row_shape,
            row_shape,
            shape(8, WIDTH),
        ],
        scratch_shapes=unit_scratch
        + [pltpu.VMEM((8, WIDTH), F32)]
        + sum_scratch
        + [pltpu.VMEM((held, 2 * WIDTH), F32)],
        compiler_params=params(),
        cost_estimate=cost(8e9, 12e6),
        name="second_back",
    )(
        second_out,
        seen,
        bn_gain,
        bn_shift,
        scatter,
        qkv_high,
        qkv_low,
        out_high,
        out_low,
        packed,
        layernorm_gains,
        layernorm_offsets,
        live_keep,
        cotangent_keep,
        *second_keep,
    )
    edge = passed_along(edge, 1)
    early = spread_rows(shared, AXES)
    middle_rows = -(-(piece + part + share_of(8, devices)) // 8) * 8
    carried, packed_keep, high_keep, low_keep, *ffn_keep = first_keep
    grad_joined, grad_mixed, pillars_out, shared = pl.pallas_call(
        functools.partial(first_ffn_back_kernel, wins=wins, ffns=ffns),
        grid=(steps,),
        in_specs=[rows_spec, whole(HALF, 2 * WIDTH), rows_spec]
        + out_specs
        + [packed_spec]
        + norm_specs
        + keep_specs[4:],
        out_specs=[rows_spec, rows_spec, rows_spec, whole(devices, middle_rows, WIDTH)],
        out_shape=[row_shape, row_shape, row_shape, shape(devices, middle_rows, WIDTH)],
        scratch_shapes=unit_scratch + [sum_scratch[0]] + sum_scratch[2:] + [pltpu.VMEM((STEP, WIDTH), F32)],
        compiler_params=params(),
        cost_estimate=cost(4e9, 6e6),
        name="first_ffn_back",
    )(
        grad_rows,
        edge,
        out_rows,
        out_high,
        out_low,
        packed,
        layernorm_gains,
        layernorm_offsets,
        *ffn_keep,
    )

    def relay(arrived, split, count, *extra):
        extra_rows = part if extra else 0
        rows = -(-(count + extra_rows) // 8) * 8
        outs = [shape(devices, rows, WIDTH)]
        if split:
            outs.append(shape(wins, split, WIDTH))
        return pl.pallas_call(
            functools.partial(relay_kernel, split=split, count=count, extra=extra_rows),
            out_shape=outs,
            compiler_params=params(),
            name="relay",
        )(arrived, *extra)

    one = share_of(8, devices)
    early, early_units = relay(early, piece, 4 * part + one, hat_product)
    early = spread_rows(early, AXES)
    early_units = spread_rows(early_units, "win")
    middle = spread_rows(shared, AXES)
    late_rows = -(-(4 * part) // 8) * 8
    grad_affine, shared, sent = pl.pallas_call(
        first_attention_back_kernel,
        grid=(steps,),
        in_specs=[rows_spec, rows_spec, rows_spec, column_spec, rows_spec, rows_spec, rows_spec]
        + qkv_specs
        + keep_specs[1:4],
        out_specs=[rows_spec, whole(devices, late_rows, WIDTH), whole(devices, 8, WIDTH)],
        out_shape=[row_shape, shape(devices, late_rows, WIDTH), shape(devices, 8, WIDTH)],
        scratch_shapes=[sum_scratch[1], sum_scratch[2], sum_scratch[0]],
        compiler_params=params(),
        cost_estimate=cost(6e9, 8e6),
        name="first_attention_back",
    )(
        grad_joined,
        grad_mixed,
        pillar_feats,
        live,
        carried,
        vfe_hat,
        vfe_slope,
        qkv_high,
        qkv_low,
        packed_keep,
        high_keep,
        low_keep,
    )
    seen = spread_rows(sent, AXES)
    late = spread_rows(shared, AXES)
    middle, late_units = relay(middle, piece, part + one)
    middle = spread_rows(middle, AXES)
    late_units = spread_rows(late_units, "win")
    late = relay(late, 0, 4 * part)[0]
    late = spread_rows(late, AXES)
    grad_feats, vfe_grads = pl.pallas_call(
        feats_back_kernel,
        out_shape=(row_shape, shape(8, WIDTH)),
        compiler_params=params(),
        cost_estimate=cost(1e8, 2e6),
        name="feats_back",
    )(grad_affine, vfe_hat, live, stats, seen, bn_gain, w_vfe)
    grads = pl.pallas_call(
        functools.partial(last_kernel, ffns=ffns),
        out_shape=(
            shape(WIDTH, WIDTH),
            shape(2, WIDTH),
            shape(2, WIDTH),
            shape(2, WIDTH, 3 * WIDTH),
            shape(2, WIDTH, WIDTH),
            shape(2, WIDTH, units),
            shape(2, units),
            shape(2, units, WIDTH),
            shape(2, WIDTH),
            shape(4, WIDTH),
            shape(4, WIDTH),
        ),
        compiler_params=params(),
        name="last",
    )(late, middle, early, late_units, early_units, stats, vfe_grads, neck, bn_gain)
    return (pillars_out, grad_feats, *grads)


def solution(mesh):
    return jax.shard_map(
        on_device,
        mesh=mesh,
        in_specs=(
            P(("win", "ffn"), None),
            P(("win", "ffn")),
            P(("win", "ffn")),
            P(),
            P(),
            P(),
            P(),
            P(),
            P(None, None, "ffn"),
            P(None, "ffn"),
            P(None, "ffn", None),
            P(),
            P(),
            P(),
            P(("win", "ffn"), None),
        ),
        out_specs=(
            P(("win", "ffn"), None),
            P(("win", "ffn"), None),
            P(),
            P(),
            P(),
            P(),
            P(),
            P(None, None, "ffn"),
            P(None, "ffn"),
            P(None, "ffn", None),
            P(),
            P(),
            P(),
        ),
        check_vma=False,
    )
```

time: 982 us -> 264 us (0.27); the launches traced: 969 us -> 263 us
  waiting for transfers between devices: 373 us -> 58.8 us
  matrix products: 177 us -> 0 us
  blocking collectives: 260 us -> 90 us
  Pallas kernels: 0 us -> 89.5 us
  other arithmetic: 73 us -> 0 us
  local copies, waits for them, and re-layouts: 58.8 us -> 7.94 us
  between operations: 16.1 us -> 0.77 us
    psum x7 -> x0, blocking collectives: 260 us -> none  [the longest x2 80.6 us: norm_stats(): lax.psum(jnp.sum(live_rows * (values - center) ** 2, axis=0), ('win', 'ff...]
    psum x2 -> x0, waiting for transfers between devices: 197 us -> none  [the longest x1 124 us: on_device(): lax.psum((local_w_vfe, stacked[0], stacked[1], stacked[5], local_ln_gain,...]
    dot_general x39 -> x0, matrix products: 177 us -> none  [the longest x6 51.7 us: window_core(): jnp.einsum('whqk,wkhe->wqhe', weights, value_rows, precision=lax.Precisio...]
    all_to_all x0 -> x7, blocking collectives: none -> 90 us  [spread_rows(): return lax.all_to_all(pieces, axes, 0, 0)]
    pallas_call x0 -> x12, Pallas kernels: none -> 89.5 us  [the longest x1 20.9 us: on_device(): pl.pallas_call(functools.partial(second_back_kernel, wins=wins, ffns=ffns...]
    all_gather x4 -> x0, waiting for transfers between devices: 82.3 us -> none  [the longest x2 42.2 us: ffn_forward(): gathered = lax.all_gather(first_norm, 'ffn', axis=0, tiled=True)]
    reduce_scatter x4 -> x0, waiting for transfers between devices: 78 us -> none  [the longest x2 49.8 us: ffn_forward(): lax.psum_scatter(matmul(hidden, back_one), 'ffn', scatter_dimension=0, ti...]
    all_to_all x0 -> x5, waiting for transfers between devices: none -> 48.8 us  [spread_rows(): return lax.all_to_all(pieces, axes, 0, 0)]
  transfers between devices with their start and end apart: 15 -> 7, of which waited for: 14 -> 7; matrix products, arithmetic and copies ran while one was open for 4% -> 0% of each run, Pallas kernels for 0% -> 5%
where the time goes in v1:
time: 264 us; the launch traced here: 263 us
  blocking collectives  90 us (34%)
  Pallas kernels  89.5 us (34%)
  waiting for transfers between devices  58.8 us (22%)
  starting transfers between devices  15.7 us (6%)
  local copies, waits for them, and re-layouts  7.94 us (3%)
    all_to_all x7, blocking collectives, spread_rows(): return lax.all_to_all(pieces, axes, 0, 0)  90 us
    all_to_all x5, waiting for transfers between devices, spread_rows(): return lax.all_to_all(pieces, axes, 0, 0)  48.8 us
    pallas_call x1, Pallas kernels, on_device(): pl.pallas_call(functools.partial(second_back_kernel, wins=wins, ffns=ffns...  20.9 us
    pallas_call x1, Pallas kernels, on_device(): pl.pallas_call(second_kernel, grid=(steps,), in_specs=[whole(row_count, W...  15.4 us
    pallas_call x1, Pallas kernels, on_device(): pl.pallas_call(first_attention_back_kernel, grid=(steps,), in_specs=[rows...  15 us
    all_to_all x5, starting transfers between devices, spread_rows(): return lax.all_to_all(pieces, axes, 0, 0)  14.7 us
    pallas_call x1, Pallas kernels, on_device(): pl.pallas_call(first_kernel, grid=(steps,), in_specs=[rows_spec, column_s...  13.8 us
    ppermute x2, waiting for transfers between devices, passed_along(): lax.ppermute(rows, AXES, [(i, (i + by) % peers) for i in range(peers)])  10 us
  transfers between devices with their start and end apart: 7, of which 7 were waited for; matrix products, arithmetic and copies ran while one was open for 0% of the time, Pallas kernels for 5%

profile of v1, /device:TPU:0, one launch (start us, length us, event | category | flops | bytes accessed | tf_op | source)
XLA Modules:
  0.0 262.6 jit_solution(4667711019453590085)
XLA Ops:
  3.5 2.9 %vfe.1 = (f32[864,128]{1,0:T(8,128)}, f32[864,1]{1,0:T(8,128)}, f32[32,8,128]{2,1,0:T(8,128)}, f32[4,264,128]{2,1,0:T(8,128)}) custom-call(f32[864,128]{1,0:T(8,128)} %feats_ref.3, f32[128,128]{1,0:T(8,128)} %weight_ref.3, s32[1,864]{1,0:T(1,128)} %reshape.32.occupied_ref, f32[2,128,64]{2,1,0:T(8,128)} %copy.28.up_ref, f32[2,64,128]{2,1,0:T(8,128)} %down_ref.1, ...), custom_call_target="tpu_custom_call" | custom-call | tf_op jit(solution)/shard_map/vfe/pallas_call | solution.py:960
  6.5 15.6 %all_to_all.60.seen_ref = f32[32,8,128]{2,1,0:T(8,128)} all-to-all(f32[32,8,128]{2,1,0:T(8,128)} %get-tuple-element.86), channel_id=1, replica_groups=mesh['win'=8,'ffn'=4] {'win','ffn'}, dimensions={0} | all-to-all | bytes 262144 | tf_op jit(solution)/shard_map/all_to_all | solution.py:917
  22.1 3.5 %all-to-all-start.1 = ((f32[4,264,128]{2,1,0:T(8,128)}), f32[4,264,128]{2,1,0:T(8,128)S(1)}, u32[]{:S(2)}, u32[]{:S(2)}) async-start(f32[4,264,128]{2,1,0:T(8,128)} %get-tuple-element.91), calls=%async_computation.1 | async-start | bytes 1081344 | tf_op jit(solution)/shard_map/all_to_all | solution.py:917
  26.2 4.1 %maps.1 = (bf16[864,944]{1,0:T(8,128)(2,1)}, bf16[3,944,288]{2,1,0:T(8,128)(2,1)}, bf16[2,128,384]{2,1,0:T(8,128)(2,1)}, bf16[2,128,384]{2,1,0:T(8,128)(2,1)}, b...) custom-call(s32[1,864]{1,0:T(1,128)} %reshape.33.source_ref, f32[2,128,384]{2,1,0:T(8,128)} %qkv_ref.1, ...), custom_call_target="tpu_custom_call" | custom-call | flops 100000000 | bytes 4000000 | tf_op jit(solution)/shard_map/maps/pallas_call | solution.py:980
  30.3 4.3 %all-to-all-done.1.packed = f32[4,264,128]{2,1,0:T(8,128)S(1)} async-done(((f32[4,264,128]{2,1,0:T(8,128)}), f32[4,264,128]{2,1,0:T(8,128)S(1)}, u32[]{:S(2)}, u32[]{:S(2)}) %all-to-all-start.1) | async-done | bytes 540704 | tf_op jit(solution)/shard_map/all_to_all | solution.py:917
  35.4 13.8 %first.1 = (f32[864,128]{1,0:T(8,128)}, f32[72,384]{1,0:T(8,128)}, f32[8,128]{1,0:T(8,128)}, f32[8,128]{1,0:T(8,128)}, f32[864,128]{1,0:T(8,128)}, /*index=5*/f3...) custom-call(f32[864,128]{1,0:T(8,128)} %get-tuple-element.84.lifted_, ...), custom_call_target="tpu_custom_call" | custom-call | flops 4000000000 | bytes 12000000 | tf_op jit(solution)/shard_map/first/pallas_call | solution.py:1034
  50.0 2.6 %collective-permute-done.edge = f32[72,384]{1,0:T(8,128)S(1)} collective-permute-done((f32[72,384]{1,0:T(8,128)}, f32[72,384]{1,0:T(8,128)S(1)}, u32[]{:S(2)}, u32[]{:S(2)}) %collective-permute-start) | collective-permute-done | bytes 110624 | tf_op jit(solution)/shard_map/ppermute | solution.py:922
  53.3 15.4 %second.1 = (f32[864,128]{1,0:T(8,128)}, f32[32,8,128]{2,1,0:T(8,128)}, f32[864,1]{1,0:T(8,128)}, f32[864,128]{1,0:T(8,128)}, f32[864,128]{1,0:T(8,128)}, /*inde...) custom-call(f32[864,128]{1,0:T(8,128)} %get-tuple-element.92.first_r, ...), custom_call_target="tpu_custom_call" | custom-call | flops 4000000000 | bytes 12000000 | tf_op jit(solution)/shard_map/second/pallas_call | solution.py:1066
  68.7 14.1 %all_to_all.61.seen_ref = f32[32,8,128]{2,1,0:T(8,128)} all-to-all(f32[32,8,128]{2,1,0:T(8,128)} %get-tuple-element.96), channel_id=1, replica_groups=mesh['win'=8,'ffn'=4] {'win','ffn'}, dimensions={0} | all-to-all | bytes 262144 | tf_op jit(solution)/shard_map/all_to_all | solution.py:917
  82.8 20.9 %second_back.1 = (f32[32,40,128]{2,1,0:T(8,128)}, f32[72,256]{1,0:T(8,128)}, f32[864,128]{1,0:T(8,128)}, f32[864,128]{1,0:T(8,128)}, f32[8,128]{1,0:T(8,128)}) custom-call(f32[864,128]{1,0:T(8,128)} %get-tuple-element.95.result, f32[32,8,128]{2,1,0:T(8,128)} %all_to_all.61.seen_ref, f32[2,128]{1,0:T(2,128)} %bn_gain.7, f32[2,128]{1,0:T(2,128)} %bn_shift.3, ...), custom_call_target="tpu_custom_call" | custom-call | flops 8000000000 | bytes 12000000 | tf_op jit(solution)/shard_map/second_back/pallas_call | solution.py:1112
  103.9 7.4 %collective-permute-done.1.edge = f32[72,256]{1,0:T(8,128)S(1)} collective-permute-done((f32[72,256]{1,0:T(8,128)}, f32[72,256]{1,0:T(8,128)S(1)}, u32[]{:S(2)}, u32[]{:S(2)}) %collective-permute-start.1) | collective-permute-done | bytes 73760 | tf_op jit(solution)/shard_map/ppermute | solution.py:922
  111.9 7.1 %first_ffn_back.1 = (f32[864,128]{1,0:T(8,128)}, f32[864,128]{1,0:T(8,128)}, f32[864,128]{1,0:T(8,128)}, f32[32,24,128]{2,1,0:T(8,128)}) custom-call(f32[864,128]{1,0:T(8,128)} %get-tuple-element.111.grad_rows, f32[72,256]{1,0:T(8,128)} %copy-done.8, f32[864,128]{1,0:T(8,128)} %get-tuple-element.113.out_rows, ...), custom_call_target="tpu_custom_call" | custom-call | flops 4000000000 | bytes 6000000 | tf_op jit(solution)/shard_map/first_ffn_back/pallas_call | solution.py:1164
  119.0 15.0 %first_attention_back.1 = (f32[864,128]{1,0:T(8,128)}, f32[32,16,128]{2,1,0:T(8,128)}, f32[32,8,128]{2,1,0:T(8,128)}) custom-call(f32[864,128]{1,0:T(8,128)} %get-tuple-element.122.grad_joined, f32[864,128]{1,0:T(8,128)} %get-tuple-element.123.grad_mixed, f32[864,128]{1,0:T(8,128)} %feats_ref.3, f32[864,1]{1,0:T(8,128)} %get-tuple-element.85.live_ref, ...), custom_call_target="tpu_custom_call" | custom-call | flops 6000000000 | bytes 8000000 | tf_op jit(solution)/shard_map/first_attention_back/pallas_call | solution.py:1209
  134.0 11.5 %all_to_all.62.seen_ref = f32[32,8,128]{2,1,0:T(8,128)} all-to-all(f32[32,8,128]{2,1,0:T(8,128)} %get-tuple-element.132), channel_id=1, replica_groups=mesh['win'=8,'ffn'=4] {'win','ffn'}, dimensions={0} | all-to-all | bytes 262144 | tf_op jit(solution)/shard_map/all_to_all | solution.py:917
  145.5 15.6 %all_to_all.63.refs_0_ = f32[32,24,128]{2,1,0:T(8,128)} all-to-all(f32[32,24,128]{2,1,0:T(8,128)S(1)} %copy-done.5), channel_id=1, replica_groups=mesh['win'=8,'ffn'=4] {'win','ffn'}, dimensions={0} | all-to-all | bytes 786432 | tf_op jit(solution)/shard_map/all_to_all | solution.py:917
  161.1 2.6 all-to-all-start.4
  163.7 1.7 relay.4
  165.4 8.9 %all-to-all-done.4.refs_0_ = f32[32,16,128]{2,1,0:T(8,128)S(1)} async-done(((f32[32,16,128]{2,1,0:T(8,128)}), f32[32,16,128]{2,1,0:T(8,128)S(1)}, u32[]{:S(2)}, u32[]{:S(2)}) %all-to-all-start.4) | async-done | bytes 262176 | tf_op jit(solution)/shard_map/all_to_all | solution.py:917
  174.3 10.9 %all_to_all.64.late_units = f32[8,16,128]{2,1,0:T(8,128)} all-to-all(f32[8,16,128]{2,1,0:T(8,128)} %get-tuple-element.140), channel_id=1, replica_groups=mesh['win'=8,'ffn'=4] {'win'}, dimensions={0} | all-to-all | bytes 131072 | tf_op jit(solution)/shard_map/all_to_all | solution.py:917
  185.1 11.5 %all_to_all.65.middle = f32[32,8,128]{2,1,0:T(8,128)} all-to-all(f32[32,8,128]{2,1,0:T(8,128)} %get-tuple-element.136), channel_id=1, replica_groups=mesh['win'=8,'ffn'=4] {'win','ffn'}, dimensions={0} | all-to-all | bytes 262144 | tf_op jit(solution)/shard_map/all_to_all | solution.py:917
  196.6 2.6 all-to-all-start.8
  199.3 1.7 relay.3
  201.0 16.2 %all-to-all-done.8.refs_0_ = f32[32,40,128]{2,1,0:T(8,128)S(1)} async-done(((f32[32,40,128]{2,1,0:T(8,128)}), f32[32,40,128]{2,1,0:T(8,128)S(1)}, u32[]{:S(2)}, u32[]{:S(2)}) %all-to-all-start.8) | async-done | bytes 655392 | tf_op jit(solution)/shard_map/all_to_all | solution.py:917
  217.2 3.4 %all-to-all-start.5 = ((f32[32,16,128]{2,1,0:T(8,128)}), f32[32,16,128]{2,1,0:T(8,128)S(1)}, u32[]{:S(2)}, u32[]{:S(2)}) async-start(f32[32,16,128]{2,1,0:T(8,128)} %relay.3), calls=%async_computation.5 | async-start | bytes 524288 | tf_op jit(solution)/shard_map/all_to_all | solution.py:917
  220.6 1.9 relay.5
  222.5 8.7 %all-to-all-done.5.late = f32[32,16,128]{2,1,0:T(8,128)S(1)} async-done(((f32[32,16,128]{2,1,0:T(8,128)}), f32[32,16,128]{2,1,0:T(8,128)S(1)}, u32[]{:S(2)}, u32[]{:S(2)}) %all-to-all-start.5) | async-done | bytes 262176 | tf_op jit(solution)/shard_map/all_to_all | solution.py:917
  231.2 10.9 %all_to_all.66.early_units = f32[8,16,128]{2,1,0:T(8,128)} all-to-all(f32[8,16,128]{2,1,0:T(8,128)} %get-tuple-element.141), channel_id=1, replica_groups=mesh['win'=8,'ffn'=4] {'win'}, dimensions={0} | all-to-all | bytes 131072 | tf_op jit(solution)/shard_map/all_to_all | solution.py:917
  242.0 2.6 all-to-all-start.9
  244.7 2.5 feats_back.1
  247.1 10.7 %all-to-all-done.9.early = f32[32,24,128]{2,1,0:T(8,128)S(1)} async-done(((f32[32,24,128]{2,1,0:T(8,128)}), f32[32,24,128]{2,1,0:T(8,128)S(1)}, u32[]{:S(2)}, u32[]{:S(2)}) %all-to-all-start.9) | async-done | bytes 393248 | tf_op jit(solution)/shard_map/all_to_all | solution.py:917
  258.6 2.4 last.1
  261.0 1.6 copy.29
  (23 shorter events, 7.4 us)
Async XLA Ops:
  0.6 24.9 %copy-start.6 = (s32[864]{0:T(1024)S(1)}, s32[864]{0:T(1024)}, u32[]{:S(2)}) copy-start(s32[864]{0:T(1024)} %param.17) | copy-start | bytes 10372
  22.1 12.5 %all-to-all-start.1 = ((f32[4,264,128]{2,1,0:T(8,128)}), f32[4,264,128]{2,1,0:T(8,128)S(1)}, u32[]{:S(2)}, u32[]{:S(2)}) async-start(f32[4,264,128]{2,1,0:T(8,128)} %get-tuple-element.91), calls=%async_computation.1 | async-start | bytes 1081344 | tf_op jit(solution)/shard_map/all_to_all | solution.py:917
  34.6 0.8 copy-start.4
  49.2 3.4 %collective-permute-start = (f32[72,384]{1,0:T(8,128)}, f32[72,384]{1,0:T(8,128)S(1)}, u32[]{:S(2)}, u32[]{:S(2)}) collective-permute-start(f32[72,384]{1,0:T(8,128)} %get-tuple-element.93), channel_id=1, source_target_pairs={{0,31},{1,0},{2,1},{3,2},{4,3},{5,4},{6,5},{7,6},{8,7},{9,8},{10,9... | collective-permute-start | bytes 331784 | tf_op jit(solution)/shard_map/ppermute | solution.py:922
  52.7 0.6 copy-start.7
  103.6 7.6 %collective-permute-start.1 = (f32[72,256]{1,0:T(8,128)}, f32[72,256]{1,0:T(8,128)S(1)}, u32[]{:S(2)}, u32[]{:S(2)}) collective-permute-start(f32[72,256]{1,0:T(8,128)} %get-tuple-element.112), channel_id=1, source_target_pairs={{0,1},{1,2},{2,3},{3,4},{4,5},{5,6},{6,7},{7,8},{8,9},{9,10},{10,1... | collective-permute-start | bytes 221192 | tf_op jit(solution)/shard_map/ppermute | solution.py:922
  111.3 0.6 copy-start.8
  119.0 26.5 %copy-start.5 = (f32[32,24,128]{2,1,0:T(8,128)S(1)}, f32[32,24,128]{2,1,0:T(8,128)}, u32[]{:S(2)}) copy-start(f32[32,24,128]{2,1,0:T(8,128)} %get-tuple-element.135) | copy-start | bytes 1179652
  161.1 13.2 %all-to-all-start.4 = ((f32[32,16,128]{2,1,0:T(8,128)}), f32[32,16,128]{2,1,0:T(8,128)S(1)}, u32[]{:S(2)}, u32[]{:S(2)}) async-start(f32[32,16,128]{2,1,0:T(8,128)} %get-tuple-element.134), calls=%async_computation.4 | async-start | bytes 524288 | tf_op jit(solution)/shard_map/all_to_all | solution.py:917
  174.3 25.0 %copy-start.3 = (f32[32,16,128]{2,1,0:T(8,128)}, f32[32,16,128]{2,1,0:T(8,128)S(1)}, u32[]{:S(2)}) copy-start(f32[32,16,128]{2,1,0:T(8,128)S(1)} %all-to-all-done.4.refs_0_) | copy-start | bytes 786436
  196.6 20.5 %all-to-all-start.8 = ((f32[32,40,128]{2,1,0:T(8,128)}), f32[32,40,128]{2,1,0:T(8,128)S(1)}, u32[]{:S(2)}, u32[]{:S(2)}) async-start(f32[32,40,128]{2,1,0:T(8,128)} %get-tuple-element.137), calls=%async_computation.8 | async-start | bytes 1310720 | tf_op jit(solution)/shard_map/all_to_all | solution.py:917
  217.2 3.4 %copy-start = (f32[32,40,128]{2,1,0:T(8,128)}, f32[32,40,128]{2,1,0:T(8,128)S(1)}, u32[]{:S(2)}) copy-start(f32[32,40,128]{2,1,0:T(8,128)S(1)} %all-to-all-done.8.refs_0_) | copy-start | bytes 1966084
  217.2 14.0 %all-to-all-start.5 = ((f32[32,16,128]{2,1,0:T(8,128)}), f32[32,16,128]{2,1,0:T(8,128)S(1)}, u32[]{:S(2)}, u32[]{:S(2)}) async-start(f32[32,16,128]{2,1,0:T(8,128)} %relay.3), calls=%async_computation.5 | async-start | bytes 524288 | tf_op jit(solution)/shard_map/all_to_all | solution.py:917
  231.2 26.7 %copy-start.2 = (f32[32,16,128]{2,1,0:T(8,128)}, f32[32,16,128]{2,1,0:T(8,128)S(1)}, u32[]{:S(2)}) copy-start(f32[32,16,128]{2,1,0:T(8,128)S(1)} %all-to-all-done.5.late) | copy-start | bytes 786436
  242.0 15.8 %all-to-all-start.9 = ((f32[32,24,128]{2,1,0:T(8,128)}), f32[32,24,128]{2,1,0:T(8,128)S(1)}, u32[]{:S(2)}, u32[]{:S(2)}) async-start(f32[32,24,128]{2,1,0:T(8,128)} %get-tuple-element.139), calls=%async_computation.9 | async-start | bytes 786432 | tf_op jit(solution)/shard_map/all_to_all | solution.py:917
  257.8 0.8 copy-start.1

commit v2 on v1

--- a/solution.py
+++ b/solution.py
@@ -33,6 +33,10 @@
 
 def rows_of(*dims):
     return pl.BlockSpec(dims, lambda i: (i,) + (0,) * (len(dims) - 1))
+
+
+def later(spec):
+    return pl.BlockSpec(spec.block_shape, lambda i: spec.index_map(i + 1))
 
 
 def share_of(rows, devices):
@@ -278,15 +282,13 @@
     return at + share
 
 
-def share_units(target, at, sum_up, sum_down, wins, ffns):
+def share_units(target, at, sum_up, sum_down, ffns):
     units = sum_up.shape[0] // ffns
-    part = 2 * units // wins
     for f in range(ffns):
         rows = slice(f * units, (f + 1) * units)
         joined = jnp.concatenate([sum_up[rows], sum_down[rows]], axis=0)
-        for w in range(wins):
-            target[w * ffns + f, at : at + part] = joined[w * part : (w + 1) * part]
-    return at + part
+        at = share_rows(target, at, joined, target.shape[0])
+    return at
 
 
 def joined_rows(table, at, count):
@@ -306,13 +308,13 @@
     feats_ref, weight_ref, occupied_ref, up_ref, down_ref, bias_ref, lifted_ref, live_ref, sent_ref, packed_ref
 ):
     devices = sent_ref.shape[0]
-    units = up_ref.shape[2]
+    units = up_ref.shape[1]
     feats = feats_ref[...]
     row_count = feats.shape[0]
     feats_halves = halves(feats)
     lifted = product(nn, feats_halves, halves(weight_ref[...]))
     lifted_ref[...] = lifted
-    live = jnp.broadcast_to(occupied_ref[...].astype(F32), (8, row_count)).T[:, :1]
+    live = jnp.broadcast_to(occupied_ref[...].astype(F32).reshape(1, row_count), (8, row_count)).T[:, :1]
     live_ref[...] = live
     count = jnp.sum(live, axis=0, keepdims=True)
     total = column_sum(live * lifted)
@@ -329,33 +331,29 @@
     )
     sent_ref[:, 0:4] = jnp.broadcast_to(stats[None], (devices, 4, WIDTH))
     share_rows(sent_ref, 4, product(tn, feats_halves, halves(moved)), devices)
-    turned = (up_ref[0].T, up_ref[1].T)
-    for to in range(packed_ref.shape[0]):
-        for one in range(2):
-            packed_ref[to, one * units : (one + 1) * units] = turned[one]
-            packed_ref[to, (2 + one) * units : (3 + one) * units] = down_ref[one]
-        packed_ref[to, 4 * units :] = jnp.zeros((8, WIDTH), F32)
-        packed_ref[to, 4 * units : 4 * units + 2, :units] = bias_ref[...]
-
-
-def maps_kernel(source_ref, qkv_ref, out_ref, gather_ref, scatter_ref, qkv_high, qkv_low, out_high, out_low):
-    row_count = source_ref.shape[1]
-    held = gather_ref.shape[1]
-    devices = lax.axis_size(AXES)
-    places = source_ref[...] - lax.axis_index(AXES) * row_count
-    places = jnp.where(places < 0, places + row_count * devices, places)
-    column = jnp.broadcast_to(places.astype(F32), (8, row_count)).T[:, :1].astype(jnp.int32)
-    for at in range(row_count // STEP):
-        rows = slice(at * STEP, (at + 1) * STEP)
-        lanes = lax.broadcasted_iota(jnp.int32, (STEP, held), 1)
-        gather_ref[rows] = (lanes == column[rows]).astype(F32).astype(BF16)
-        down = lax.broadcasted_iota(jnp.int32, (held, STEP), 0)
-        scatter_ref[at] = (down == places[:, rows]).astype(F32).astype(BF16)
+    for one in range(2):
+        packed_ref[one * units : (one + 1) * units] = up_ref[one]
+        packed_ref[(2 + one) * units : (3 + one) * units] = down_ref[one]
+    packed_ref[4 * units :] = jnp.zeros((8, WIDTH), F32)
+    packed_ref[4 * units : 4 * units + 2, :units] = bias_ref[...]
+
+
+def places_of(source_ref):
+    row_count = source_ref.shape[0]
+    places = source_ref[...].reshape(1, row_count) - lax.axis_index(AXES) * row_count
+    return jnp.where(places < 0, places + row_count * lax.axis_size(AXES), places)
+
+
+def one_hot(former, latter):
+    return (former == latter).astype(F32).astype(BF16)
+
+
+def split_kernel(qkv_ref, out_ref, qkv_high, qkv_low, out_high, out_low):
     qkv_high[...], qkv_low[...] = halves(qkv_ref[...])
     out_high[...], out_low[...] = halves(out_ref[...])
 
 
-def vfe_stats(seen_ref, gain_ref, shift_ref, stats_ref, product_ref):
+def vfe_stats(seen_ref, stats_ref, product_ref):
     counts, totals, squares, lives = (seen_ref[:, at] for at in range(4))
     count = column_sum(counts)
     center = column_sum(totals) / count
@@ -376,50 +374,24 @@
         product_ref[at : at + 1] = rate * column_sum(seen_ref[:, 4 + at] + picked * moves)
 
 
-def first_kernel(
-    lifted_ref,
-    live_ref,
-    cotangent_ref,
-    seen_ref,
-    bn_gain,
-    bn_shift,
-    qkv_high,
-    qkv_low,
-    out_high,
-    out_low,
-    packed,
-    back_bias,
-    gains,
-    offsets,
-    result,
-    edge,
-    stats,
-    hat_product,
-    vfe_hat,
-    vfe_slope,
-    carried,
-    packed_keep,
-    high_keep,
-    low_keep,
-    mixed_keep,
-    hat_one,
-    rate_one,
-    hidden_keep,
-    slope,
-    hat_two,
-    rate_two,
-    up_high,
-    up_low,
-    down_high,
-    down_low,
-    bias,
-):
-    at = pl.program_id(0)
-
-    @pl.when(at == 0)
+def first_kernel(*refs, tail):
+    lifted_ref, live_ref = refs[:2]
+    bn_gain, bn_shift, qkv_high, qkv_low, out_high, out_low, packed, back_bias, gains, offsets = refs[2:12]
+    if tail:
+        stats = refs[12]
+        refs = refs[27:]
+    else:
+        cotangent_ref, seen_ref, edge, stats, hat_product = refs[12:17]
+        refs = refs[17:]
+    result, vfe_hat, vfe_slope, carried = refs[:4]
+    saved = refs[4:14]
+    up_high, up_low, down_high, down_low, bias = refs[14:]
+
+    @pl.when(pl.program_id(0) == 0)
     def _():
         unpack_weights(packed, 0, up_high, up_low, down_high, down_low, bias)
-        vfe_stats(seen_ref, bn_gain, bn_shift, stats, hat_product)
+        if not tail:
+            vfe_stats(seen_ref, stats, hat_product)
 
     hat = (lifted_ref[...] - stats[1:2]) * stats[2:3]
     values, steep = gelu_parts(hat * bn_gain[0:1] + bn_shift[0:1])
@@ -443,12 +415,10 @@
             gains,
             offsets,
         ),
-        (packed_keep, high_keep, low_keep, mixed_keep, hat_one, rate_one, hidden_keep, slope, hat_two, rate_two),
+        saved,
     )
     result[...] = rows
-
-    @pl.when(at == 0)
-    def _():
+    if not tail:
         edge[:, :WIDTH] = rows[:HALF]
         edge[:, WIDTH : 2 * WIDTH] = cotangent_ref[:HALF]
         edge[:, 2 * WIDTH :] = jnp.broadcast_to(live[:HALF], (HALF, WIDTH))
@@ -459,7 +429,7 @@
     cotangent_ref,
     live_ref,
     edge,
-    gather_ref,
+    source_ref,
     qkv_high,
     qkv_low,
     out_high,
@@ -490,6 +460,7 @@
     bias,
     table,
     sums,
+    column,
 ):
     at = pl.program_id(0)
     row_count = first_ref.shape[0]
@@ -513,8 +484,11 @@
         table[row_count:, 3 * WIDTH : 4 * WIDTH] = low[:, WIDTH : 2 * WIDTH]
         table[row_count:, 4 * WIDTH :] = high[:, 2 * WIDTH :]
         sums[...] = jnp.zeros(sums.shape, F32)
-
-    gathered = nn(gather_ref[...], table[...])
+        places = jnp.broadcast_to(places_of(source_ref).astype(F32), (8, row_count))
+        column[...] = places.T[:, :1].astype(jnp.int32)
+
+    lanes = lax.broadcasted_iota(jnp.int32, (STEP, table.shape[0]), 1)
+    gathered = nn(one_hot(lanes, column[pl.ds(at * STEP, STEP)]), table[...])
     values = gathered[:, :WIDTH] + gathered[:, WIDTH : 2 * WIDTH]
     live = gathered[:, 4 * WIDTH :]
     grad = live * (gathered[:, 2 * WIDTH : 3 * WIDTH] + gathered[:, 3 * WIDTH : 4 * WIDTH])
@@ -576,7 +550,7 @@
     seen_ref,
     bn_gain,
     bn_shift,
-    scatter_ref,
+    source_ref,
     qkv_high,
     qkv_low,
     out_high,
@@ -602,20 +576,20 @@
     grad_rows,
     out_rows,
     neck,
+    small,
     up_high,
     up_low,
     down_high,
     down_low,
     bias,
     stats,
-    small,
     sum_qkv,
     sum_out,
     sum_up,
     sum_down,
     placed,
+    places_ref,
     *,
-    wins,
     ffns,
 ):
     at = pl.program_id(0)
@@ -638,6 +612,9 @@
         neck[0:2] = stats[3:5]
         for held in (small, sum_qkv, sum_out, sum_up, sum_down, placed):
             held[...] = jnp.zeros(held.shape, F32)
+        places = places_of(source_ref)
+        for step in range(places_ref.shape[0]):
+            places_ref[step] = places[:, step * STEP : (step + 1) * STEP]
 
     live = live_keep[...]
     rate = stats[2:3]
@@ -670,7 +647,8 @@
         sum_qkv,
     )
     pieces = halves(grad_values) + halves(neck_rows)
-    moved = nn(scatter_ref[0], jnp.concatenate(pieces, axis=1))
+    down = lax.broadcasted_iota(jnp.int32, (placed.shape[0], STEP), 0)
+    moved = nn(one_hot(down, places_ref[at]), jnp.concatenate(pieces, axis=1))
     placed[:, :WIDTH] += moved[:, :WIDTH] + moved[:, WIDTH : 2 * WIDTH]
     placed[:, WIDTH:] += moved[:, 2 * WIDTH : 3 * WIDTH] + moved[:, 3 * WIDTH :]
 
@@ -679,69 +657,47 @@
         grad_rows[...] = placed[:row_count, :WIDTH]
         out_rows[...] = placed[:row_count, WIDTH:]
         edge[...] = placed[row_count : row_count + HALF]
-        devices = wins * ffns
+        devices = shared.shape[0]
         shared[...] = jnp.zeros(shared.shape, F32)
-        row = share_units(shared, 0, sum_up, sum_down, wins, ffns)
+        row = share_units(shared, 0, sum_up, sum_down, ffns)
         for block in range(3):
             row = share_rows(shared, row, sum_qkv[:, block * WIDTH : (block + 1) * WIDTH], devices)
-        row = share_rows(shared, row, sum_out, devices)
-        share_rows(shared, row, small, devices)
-
-
-def first_ffn_back_kernel(
-    grad_rows,
-    edge,
-    out_rows,
-    out_high,
-    out_low,
-    packed,
-    gains,
-    offsets,
-    mixed_keep,
-    hat_one,
-    rate_one,
-    hidden_keep,
-    slope,
-    hat_two,
-    rate_two,
-    grad_joined,
-    grad_mixed,
-    pillars,
-    shared,
-    up_high,
-    up_low,
-    down_high,
-    down_low,
-    bias,
-    small,
-    sum_out,
-    sum_up,
-    sum_down,
-    grad_step,
-    *,
-    wins,
-    ffns,
-):
-    at = pl.program_id(0)
-
-    @pl.when(at == 0)
+        share_rows(shared, row, sum_out, devices)
+
+
+def first_ffn_back_kernel(*refs, tail):
+    grad_rows, out_high, out_low, packed, gains, offsets = refs[:6]
+    keeps = refs[6:13]
+    refs = refs[13:]
+    if tail:
+        edge, out_rows = refs[:2]
+        held_sums = refs[2:6]
+        grad_joined, grad_mixed, pillars = refs[8:11]
+        sums = refs[11:15]
+        refs = refs[15:]
+    else:
+        grad_joined, grad_mixed = refs[:2]
+        sums = refs[2:6]
+        refs = refs[6:]
+    up_high, up_low, down_high, down_low, bias = refs[:5]
+    grad = grad_rows
+
+    @pl.when(pl.program_id(0) == 0)
     def _():
         unpack_weights(packed, 0, up_high, up_low, down_high, down_low, bias)
-        for held in (small, sum_out, sum_up, sum_down):
-            held[...] = jnp.zeros(held.shape, F32)
-
-    grad_step[...] = grad_rows[...]
-    pillars[...] = out_rows[...]
-
-    @pl.when(at == 0)
-    def _():
-        grad_step[:HALF] = edge[:, :WIDTH]
+        for at, held in enumerate(sums):
+            held[...] = held_sums[at][...] if tail else jnp.zeros(held.shape, F32)
+
+    if tail:
+        grad = refs[5]
+        grad[...] = grad_rows[...]
+        grad[:HALF] = edge[:, :WIDTH]
+        pillars[...] = out_rows[...]
         pillars[:HALF] = edge[:, WIDTH:]
-
     joined, mixed = ffn_rows_back(
         0,
-        grad_step[...],
-        (mixed_keep, hat_one, rate_one, hidden_keep, slope, hat_two, rate_two),
+        grad[...],
+        keeps,
         (
             (out_high[0], out_low[0]),
             (up_high[...], up_low[...]),
@@ -749,17 +705,10 @@
             gains,
             offsets,
         ),
-        (small, sum_out, sum_up, sum_down),
+        sums,
     )
     grad_joined[...] = joined
     grad_mixed[...] = mixed
-
-    @pl.when(at == pl.num_programs(0) - 1)
-    def _():
-        shared[...] = jnp.zeros(shared.shape, F32)
-        row = share_units(shared, 0, sum_up, sum_down, wins, ffns)
-        row = share_rows(shared, row, sum_out, wins * ffns)
-        share_rows(shared, row, small, wins * ffns)
 
 
 def first_attention_back_kernel(
@@ -775,12 +724,18 @@
     packed_keep,
     high_keep,
     low_keep,
+    small_second,
+    small_ffn,
+    sum_out,
+    sum_up,
+    sum_down,
     grad_affine,
     shared,
-    sent,
     sum_qkv,
     sum_feats,
     small,
+    *,
+    ffns,
 ):
     at = pl.program_id(0)
 
@@ -809,31 +764,48 @@
     def _():
         devices = shared.shape[0]
         shared[...] = jnp.zeros(shared.shape, F32)
-        row = 0
+        row = share_units(shared, 0, sum_up, sum_down, ffns)
         for block in range(3):
             row = share_rows(shared, row, sum_qkv[:, block * WIDTH : (block + 1) * WIDTH], devices)
-        share_rows(shared, row, sum_feats, devices)
-        sent[...] = jnp.broadcast_to(small[...][None], sent.shape)
-
-
-def relay_kernel(*refs, split, count, extra):
-    arrived = refs[0]
-    total = jnp.sum(arrived[...], axis=0)
-    outs = refs[2:] if extra else refs[1:]
-    if split:
-        outs[1][...] = jnp.broadcast_to(total[:split][None], outs[1].shape)
-    rows = total[split : split + count]
-    if extra:
-        rows = jnp.concatenate([rows, refs[1][:extra]], axis=0)
-    room = outs[0].shape[1]
+        row = share_rows(shared, row, sum_out, devices)
+        row = share_rows(shared, row, small_second[...], devices)
+        row = share_rows(shared, row, small_ffn[...], devices)
+        row = share_rows(shared, row, sum_feats, devices)
+        shared[:, row : row + 2] = jnp.broadcast_to(small[0:2][None], (devices, 2, WIDTH))
+
+
+def relay_kernel(early, late, hat_product, stats, bn_gain, returned, vfe_grads, *, ffns, counts):
+    unit_rows, early_rows, late_rows, part = counts
+    devices = returned.shape[0]
+    early_total = jnp.sum(early[...], axis=0)
+    late_total = jnp.sum(late[...], axis=0)
+    begin = ffns * unit_rows
+    end = begin + late_rows
+    gain, shift = late_total[end + part : end + part + 1], late_total[end + part + 1 : end + part + 2]
+    lanes = lax.broadcasted_iota(jnp.int32, (part, WIDTH), 1)
+    mine = lax.axis_index(AXES) * part + lax.broadcasted_iota(jnp.int32, (part, WIDTH), 0)
+    live_sum = jnp.sum(jnp.where(lanes == mine, stats[3:4], 0.0), axis=1, keepdims=True)
+    grad_w_vfe = stats[2:3] * bn_gain[0:1] * (
+        late_total[end : end + part] - (hat_product[:part] * gain + live_sum * shift) / stats[0:1]
+    )
+    rows = jnp.concatenate(
+        [early_total[begin : begin + early_rows], late_total[begin:end], grad_w_vfe], axis=0
+    )
+    room = returned.shape[1] - 2 * unit_rows
     if rows.shape[0] < room:
         rows = jnp.concatenate([rows, jnp.zeros((room - rows.shape[0], WIDTH), F32)], axis=0)
-    outs[0][...] = jnp.broadcast_to(rows[:room][None], outs[0].shape)
-
-
-def feats_back_kernel(grad_affine, vfe_hat, live_ref, stats, seen_ref, bn_gain, weight_ref, grad_feats, vfe_grads):
-    sums = jnp.sum(seen_ref[...], axis=0)
-    vfe_grads[...] = sums
+    returned[:, 2 * unit_rows :] = jnp.broadcast_to(rows[None], (devices,) + rows.shape)
+    for device in range(devices):
+        block = device % ffns
+        for at, total in enumerate((early_total, late_total)):
+            returned[device, at * unit_rows : (at + 1) * unit_rows] = total[
+                block * unit_rows : (block + 1) * unit_rows
+            ]
+    vfe_grads[...] = jnp.concatenate([gain, shift, jnp.zeros((6, WIDTH), F32)], axis=0)
+
+
+def feats_back_kernel(grad_affine, vfe_hat, live_ref, stats, vfe_grads, bn_gain, weight_ref, grad_feats):
+    sums = vfe_grads[...]
     scale = stats[2:3] * bn_gain[0:1]
     grad = scale * (
         grad_affine[...]
@@ -843,15 +815,9 @@
 
 
 def last_kernel(
-    late,
-    middle,
-    early,
-    late_units,
-    early_units,
-    stats,
+    returned,
     vfe_grads,
     neck,
-    bn_gain,
     grad_w_vfe,
     grad_bn_gain,
     grad_bn_shift,
@@ -866,28 +832,28 @@
     *,
     ffns,
 ):
-    devices = late.shape[0]
+    devices = returned.shape[0]
+    units = grad_w_in.shape[1]
     part = share_of(WIDTH, devices)
-    units = grad_w_in.shape[2]
-    wins = late_units.shape[0]
-    piece = 2 * units // wins
-    for block in range(3):
-        lanes = slice(block * WIDTH, (block + 1) * WIDTH)
-        grad_w_qkv[0, :, lanes] = joined_rows(late, block * part, WIDTH)
-        grad_w_qkv[1, :, lanes] = joined_rows(early, block * part, WIDTH)
-    feats_sum = joined_rows(late, 3 * part, WIDTH)
-    grad_w_out[0] = joined_rows(middle, 0, WIDTH)
-    grad_w_out[1] = joined_rows(early, 3 * part, WIDTH)
-    small_rows = 8
-    one = share_of(small_rows, devices)
-    smalls = (
-        joined_rows(middle, part, small_rows),
-        joined_rows(early, 4 * part, small_rows),
-    )
-    hat_sum = joined_rows(early, 4 * part + one, WIDTH)
+    unit_rows = share_of(2 * units, devices)
+    at = 0
+
+    def take(count):
+        nonlocal at
+        rows = joined_rows(returned, at, count)
+        at += share_of(count, devices)
+        return rows
+
+    blocks = [take(2 * units) for layer in range(2)]
     mine = lax.rem(lax.axis_index(AXES), ffns)
-    for layer in range(2):
-        small = smalls[layer]
+    for layer in (1, 0):
+        grad_w_in[layer] = blocks[1 - layer][:units]
+        grad_w_back[layer] = blocks[1 - layer][units:]
+        for block in range(3):
+            grad_w_qkv[layer, :, block * WIDTH : (block + 1) * WIDTH] = take(WIDTH)
+        grad_w_out[layer] = take(WIDTH)
+    for layer in (1, 0):
+        small = take(8)
         grad_b_back[layer : layer + 1] = small[0:1]
         grad_ln_gain[2 * layer : 2 * layer + 1] = small[1:2]
         grad_ln_shift[2 * layer : 2 * layer + 1] = small[2:3]
@@ -898,19 +864,11 @@
             row, lane = divmod(f * units, WIDTH)
             held = jnp.where(mine == f, small[5 + row : 6 + row, lane : lane + units], held)
         grad_b_in[layer : layer + 1] = held
-        table = (late_units, early_units)[layer]
-        joined = joined_rows(table, 0, 2 * units)
-        grad_w_in[layer] = joined[:units].T
-        grad_w_back[layer] = joined[units:]
-    gain, shift = vfe_grads[0:1], vfe_grads[1:2]
-    grad_bn_gain[0:1] = gain
+    grad_w_vfe[...] = take(WIDTH)
+    grad_bn_gain[0:1] = vfe_grads[0:1]
     grad_bn_gain[1:2] = neck[0:1]
-    grad_bn_shift[0:1] = shift
+    grad_bn_shift[0:1] = vfe_grads[1:2]
     grad_bn_shift[1:2] = neck[1:2]
-    live_sum = jnp.broadcast_to(stats[3:4], (8, WIDTH)).T[:, :1]
-    grad_w_vfe[...] = stats[2:3] * bn_gain[0:1] * (
-        feats_sum - (hat_sum * gain + live_sum * shift) / stats[0:1]
-    )
 
 
 def spread_rows(pieces, axes):
@@ -963,34 +921,32 @@
             shape(row_count, WIDTH),
             shape(row_count, 1),
             shape(devices, stats_rows, WIDTH),
-            shape(ffns, 4 * units + 8, WIDTH),
+            shape(4 * units + 8, WIDTH),
         ),
         compiler_params=params(),
         name="vfe",
     )(
         pillar_feats,
         w_vfe,
-        occupied.reshape(1, row_count),
-        up_weight_matrix,
+        occupied,
+        up_weight_matrix.transpose(0, 2, 1),
         down_weight_matrix,
         up_bias_rows,
     )
     seen = spread_rows(sent, AXES)
-    packed = spread_rows(packed, "ffn")
-    gather, scatter, qkv_high, qkv_low, out_high, out_low = pl.pallas_call(
-        maps_kernel,
+    packed = lax.all_gather(packed, "ffn", axis=0, tiled=False)
+    qkv_high, qkv_low, out_high, out_low = pl.pallas_call(
+        split_kernel,
         out_shape=(
-            shape(row_count, held, dtype=BF16),
-            shape(steps, held, STEP, dtype=BF16),
             shape(2, WIDTH, 3 * WIDTH, dtype=BF16),
             shape(2, WIDTH, 3 * WIDTH, dtype=BF16),
             shape(2, WIDTH, WIDTH, dtype=BF16),
             shape(2, WIDTH, WIDTH, dtype=BF16),
         ),
         compiler_params=params(),
-        cost_estimate=cost(1e8, 4e6),
-        name="maps",
-    )(shifted_source_rows.reshape(1, row_count), query_key_value_weight, attention_output_weight)
+        cost_estimate=cost(1e6, 1e6),
+        name="split",
+    )(query_key_value_weight, attention_output_weight)
 
     rows_spec = rows_of(STEP, WIDTH)
     column_spec = rows_of(STEP, 1)
@@ -1031,26 +987,10 @@
         row_shape,
     ]
 
-    first_out, edge, stats, hat_product, vfe_hat, vfe_slope, *first_keep = pl.pallas_call(
-        first_kernel,
-        grid=(steps,),
-        in_specs=[rows_spec, column_spec, rows_spec, seen_spec, pair_spec, pair_spec]
-        + qkv_specs
-        + out_specs
-        + [packed_spec, pair_spec]
-        + norm_specs,
-        out_specs=[rows_spec, whole(HALF, 3 * WIDTH), eight_spec, eight_spec, rows_spec, rows_spec] + keep_specs,
-        out_shape=[row_shape, shape(HALF, 3 * WIDTH), shape(8, WIDTH), shape(8, WIDTH), row_shape, row_shape]
-        + keep_shapes,
-        scratch_shapes=unit_scratch,
-        compiler_params=params(),
-        cost_estimate=cost(4e9, 12e6),
-        name="first",
-    )(
-        lifted,
-        live,
-        cotangent,
-        seen,
+    first_arrays = [row_shape, row_shape, row_shape] + keep_shapes
+    first_specs = [rows_spec, rows_spec, rows_spec] + keep_specs
+    first_shared = [pair_spec, pair_spec] + qkv_specs + out_specs + [packed_spec, pair_spec] + norm_specs
+    first_held = (
         bn_gain,
         bn_shift,
         qkv_high,
@@ -1062,7 +1002,34 @@
         layernorm_gains,
         layernorm_offsets,
     )
-    edge = passed_along(edge, -1)
+    edge, stats, hat_product, *first_arrays_out = pl.pallas_call(
+        functools.partial(first_kernel, tail=False),
+        grid=(1,),
+        in_specs=[rows_spec, column_spec] + first_shared + [rows_spec, seen_spec],
+        out_specs=[whole(HALF, 3 * WIDTH), eight_spec, eight_spec] + first_specs,
+        out_shape=[shape(HALF, 3 * WIDTH), shape(8, WIDTH), shape(8, WIDTH)] + first_arrays,
+        scratch_shapes=unit_scratch,
+        compiler_params=params(),
+        cost_estimate=cost(1e9, 4e6),
+        name="first",
+    )(lifted, live, *first_held, cotangent, seen)
+    arrived = passed_along(edge, -1)
+    first_out, vfe_hat, vfe_slope, *first_keep = pl.pallas_call(
+        functools.partial(first_kernel, tail=True),
+        grid=(steps - 1,),
+        in_specs=[later(spec) for spec in (rows_spec, column_spec)]
+        + first_shared
+        + [eight_spec]
+        + [pl.BlockSpec(memory_space=pl.ANY)] * len(first_arrays),
+        out_specs=[later(spec) for spec in first_specs],
+        out_shape=first_arrays,
+        input_output_aliases={13 + at: at for at in range(len(first_arrays))},
+        scratch_shapes=unit_scratch,
+        compiler_params=params(),
+        cost_estimate=cost(2e9, 8e6),
+        name="first_rest",
+    )(lifted, live, *first_held, stats, *first_arrays_out)
+    edge = arrived
     second_out, sent, live_keep, cotangent_keep, *second_keep = pl.pallas_call(
         second_kernel,
         grid=(steps,),
@@ -1071,7 +1038,7 @@
             whole(row_count, WIDTH),
             whole(row_count, 1),
             whole(HALF, 3 * WIDTH),
-            rows_of(STEP, held),
+            whole(row_count),
         ]
         + qkv_specs
         + out_specs
@@ -1080,7 +1047,7 @@
         out_specs=[rows_spec, whole(devices, 8, WIDTH), column_spec, rows_spec] + keep_specs,
         out_shape=[row_shape, shape(devices, 8, WIDTH), shape(row_count, 1), row_shape] + keep_shapes,
         scratch_shapes=unit_scratch
-        + [pltpu.VMEM((held, 5 * WIDTH), BF16), pltpu.VMEM((8, WIDTH), F32)],
+        + [pltpu.VMEM((held, 5 * WIDTH), BF16), pltpu.VMEM((8, WIDTH), F32), pltpu.VMEM((row_count, 1), jnp.int32)],
         compiler_params=params(),
         cost_estimate=cost(4e9, 12e6),
         name="second",
@@ -1089,7 +1056,7 @@
         cotangent,
         live,
         edge,
-        gather,
+        shifted_source_rows,
         qkv_high,
         qkv_low,
         out_high,
@@ -1100,8 +1067,11 @@
         layernorm_offsets,
     )
     seen = spread_rows(sent, AXES)
-    piece = 2 * units // wins
-    early_rows = -(-(piece + 4 * part + share_of(8, devices)) // 8) * 8
+    piece = share_of(2 * units, devices)
+    rest = 4 * part + 2 * share_of(8, devices)
+    early_rows = -(-(ffns * piece + 4 * part) // 8) * 8
+    late_rows = -(-(ffns * piece + rest + part + 2) // 8) * 8
+    returned_rows = -(-(2 * piece + 4 * part + rest + part) // 8) * 8
     sum_scratch = [
         pltpu.VMEM((8, WIDTH), F32),
         pltpu.VMEM((WIDTH, 3 * WIDTH), F32),
@@ -1109,10 +1079,10 @@
         pltpu.VMEM((hidden, WIDTH), F32),
         pltpu.VMEM((hidden, WIDTH), F32),
     ]
-    shared, edge, grad_rows, out_rows, neck = pl.pallas_call(
-        functools.partial(second_back_kernel, wins=wins, ffns=ffns),
+    shared, edge, grad_rows, out_rows, neck, small = pl.pallas_call(
+        functools.partial(second_back_kernel, ffns=ffns),
         grid=(steps,),
-        in_specs=[rows_spec, whole(devices, 8, WIDTH), pair_spec, pair_spec, rows_of(1, held, STEP)]
+        in_specs=[rows_spec, whole(devices, 8, WIDTH), pair_spec, pair_spec, whole(row_count)]
         + qkv_specs
         + out_specs
         + [packed_spec]
@@ -1125,6 +1095,7 @@
             whole(row_count, WIDTH),
             whole(row_count, WIDTH),
             eight_spec,
+            eight_spec,
         ],
         out_shape=[
             shape(devices, early_rows, WIDTH),
@@ -1132,11 +1103,12 @@
             row_shape,
             row_shape,
             shape(8, WIDTH),
+            shape(8, WIDTH),
         ],
         scratch_shapes=unit_scratch
         + [pltpu.VMEM((8, WIDTH), F32)]
-        + sum_scratch
-        + [pltpu.VMEM((held, 2 * WIDTH), F32)],
+        + sum_scratch[1:]
+        + [pltpu.VMEM((held, 2 * WIDTH), F32), pltpu.VMEM((steps, 1, STEP), jnp.int32)],
         compiler_params=params(),
         cost_estimate=cost(8e9, 12e6),
         name="second_back",
@@ -1145,7 +1117,7 @@
         seen,
         bn_gain,
         bn_shift,
-        scatter,
+        shifted_source_rows,
         qkv_high,
         qkv_low,
         out_high,
@@ -1157,63 +1129,52 @@
         cotangent_keep,
         *second_keep,
     )
-    edge = passed_along(edge, 1)
+    arrived = passed_along(edge, 1)
+    carried, packed_keep, high_keep, low_keep, *ffn_keep = first_keep
+    back_specs = [rows_spec] + out_specs + [packed_spec] + norm_specs + keep_specs[4:]
+    back_held = (grad_rows, out_high, out_low, packed, layernorm_gains, layernorm_offsets, *ffn_keep)
+    sum_shapes = [shape(8, WIDTH), shape(WIDTH, WIDTH), shape(hidden, WIDTH), shape(hidden, WIDTH)]
+    sum_specs = [whole(*held.shape) for held in sum_shapes]
+    grad_joined, grad_mixed, *sums = pl.pallas_call(
+        functools.partial(first_ffn_back_kernel, tail=False),
+        grid=(steps - 1,),
+        in_specs=[later(rows_spec)]
+        + back_specs[1:6]
+        + [later(spec) for spec in back_specs[6:]],
+        out_specs=[later(rows_spec), later(rows_spec)] + sum_specs,
+        out_shape=[row_shape, row_shape] + sum_shapes,
+        scratch_shapes=unit_scratch,
+        compiler_params=params(),
+        cost_estimate=cost(2e9, 4e6),
+        name="first_ffn_back",
+    )(*back_held)
+    shared, arrived, grad_joined = lax.optimization_barrier((shared, arrived, grad_joined))
     early = spread_rows(shared, AXES)
-    middle_rows = -(-(piece + part + share_of(8, devices)) // 8) * 8
-    carried, packed_keep, high_keep, low_keep, *ffn_keep = first_keep
-    grad_joined, grad_mixed, pillars_out, shared = pl.pallas_call(
-        functools.partial(first_ffn_back_kernel, wins=wins, ffns=ffns),
-        grid=(steps,),
-        in_specs=[rows_spec, whole(HALF, 2 * WIDTH), rows_spec]
-        + out_specs
-        + [packed_spec]
-        + norm_specs
-        + keep_specs[4:],
-        out_specs=[rows_spec, rows_spec, rows_spec, whole(devices, middle_rows, WIDTH)],
-        out_shape=[row_shape, row_shape, row_shape, shape(devices, middle_rows, WIDTH)],
-        scratch_shapes=unit_scratch + [sum_scratch[0]] + sum_scratch[2:] + [pltpu.VMEM((STEP, WIDTH), F32)],
+    grad_joined, grad_mixed, pillars_out, *sums = pl.pallas_call(
+        functools.partial(first_ffn_back_kernel, tail=True),
+        grid=(1,),
+        in_specs=back_specs
+        + [whole(HALF, 2 * WIDTH), rows_spec]
+        + sum_specs
+        + [pl.BlockSpec(memory_space=pl.ANY)] * 2,
+        out_specs=[rows_spec] * 3 + sum_specs,
+        out_shape=[row_shape] * 3 + sum_shapes,
+        input_output_aliases={14: 2, 19: 0, 20: 1},
+        scratch_shapes=unit_scratch + [pltpu.VMEM((STEP, WIDTH), F32)],
         compiler_params=params(),
-        cost_estimate=cost(4e9, 6e6),
-        name="first_ffn_back",
-    )(
-        grad_rows,
-        edge,
-        out_rows,
-        out_high,
-        out_low,
-        packed,
-        layernorm_gains,
-        layernorm_offsets,
-        *ffn_keep,
-    )
-
-    def relay(arrived, split, count, *extra):
-        extra_rows = part if extra else 0
-        rows = -(-(count + extra_rows) // 8) * 8
-        outs = [shape(devices, rows, WIDTH)]
-        if split:
-            outs.append(shape(wins, split, WIDTH))
-        return pl.pallas_call(
-            functools.partial(relay_kernel, split=split, count=count, extra=extra_rows),
-            out_shape=outs,
-            compiler_params=params(),
-            name="relay",
-        )(arrived, *extra)
-
-    one = share_of(8, devices)
-    early, early_units = relay(early, piece, 4 * part + one, hat_product)
-    early = spread_rows(early, AXES)
-    early_units = spread_rows(early_units, "win")
-    middle = spread_rows(shared, AXES)
-    late_rows = -(-(4 * part) // 8) * 8
-    grad_affine, shared, sent = pl.pallas_call(
-        first_attention_back_kernel,
+        cost_estimate=cost(1e9, 2e6),
+        name="first_ffn_back_edge",
+    )(*back_held, arrived, out_rows, *sums, grad_joined, grad_mixed)
+    grad_affine, shared = pl.pallas_call(
+        functools.partial(first_attention_back_kernel, ffns=ffns),
         grid=(steps,),
         in_specs=[rows_spec, rows_spec, rows_spec, column_spec, rows_spec, rows_spec, rows_spec]
         + qkv_specs
-        + keep_specs[1:4],
-        out_specs=[rows_spec, whole(devices, late_rows, WIDTH), whole(devices, 8, WIDTH)],
-        out_shape=[row_shape, shape(devices, late_rows, WIDTH), shape(devices, 8, WIDTH)],
+        + keep_specs[1:4]
+        + [eight_spec]
+        + sum_specs,
+        out_specs=[rows_spec, whole(devices, late_rows, WIDTH)],
+        out_shape=[row_shape, shape(devices, late_rows, WIDTH)],
         scratch_shapes=[sum_scratch[1], sum_scratch[2], sum_scratch[0]],
         compiler_params=params(),
         cost_estimate=cost(6e9, 8e6),
@@ -1231,22 +1192,26 @@
         packed_keep,
         high_keep,
         low_keep,
-    )
-    seen = spread_rows(sent, AXES)
+        small,
+        *sums,
+    )
+    early, shared = lax.optimization_barrier((early, shared))
     late = spread_rows(shared, AXES)
-    middle, late_units = relay(middle, piece, part + one)
-    middle = spread_rows(middle, AXES)
-    late_units = spread_rows(late_units, "win")
-    late = relay(late, 0, 4 * part)[0]
-    late = spread_rows(late, AXES)
-    grad_feats, vfe_grads = pl.pallas_call(
+    returned, vfe_grads = pl.pallas_call(
+        functools.partial(relay_kernel, ffns=ffns, counts=(piece, 4 * part, rest, part)),
+        out_shape=(shape(devices, returned_rows, WIDTH), shape(8, WIDTH)),
+        compiler_params=params(),
+        name="relay",
+    )(early, late, hat_product, stats, bn_gain)
+    returned = spread_rows(returned, AXES)
+    grad_feats = pl.pallas_call(
         feats_back_kernel,
-        out_shape=(row_shape, shape(8, WIDTH)),
+        out_shape=row_shape,
         compiler_params=params(),
         cost_estimate=cost(1e8, 2e6),
         name="feats_back",
-    )(grad_affine, vfe_hat, live, stats, seen, bn_gain, w_vfe)
-    grads = pl.pallas_call(
+    )(grad_affine, vfe_hat, live, stats, vfe_grads, bn_gain, w_vfe)
+    grads = list(pl.pallas_call(
         functools.partial(last_kernel, ffns=ffns),
         out_shape=(
             shape(WIDTH, WIDTH),
@@ -1254,7 +1219,7 @@
             shape(2, WIDTH),
             shape(2, WIDTH, 3 * WIDTH),
             shape(2, WIDTH, WIDTH),
-            shape(2, WIDTH, units),
+            shape(2, units, WIDTH),
             shape(2, units),
             shape(2, units, WIDTH),
             shape(2, WIDTH),
@@ -1263,7 +1228,8 @@
         ),
         compiler_params=params(),
         name="last",
-    )(late, middle, early, late_units, early_units, stats, vfe_grads, neck, bn_gain)
+    )(returned, vfe_grads, neck))
+    grads[5] = grads[5].transpose(0, 2, 1)
     return (pillars_out, grad_feats, *grads)
 
 

time: 264 us -> 175 us (0.66)
  blocking collectives: 90 us -> 45 us
  waiting for transfers between devices: 58.8 us -> 20.3 us
  local copies, waits for them, and re-layouts: 7.94 us -> 2.18 us
  starting transfers between devices: 15.7 us -> 18.5 us
    all_to_all x7 -> x2, blocking collectives: 90 us -> 35.4 us  [spread_rows(): return lax.all_to_all(pieces, axes, 0, 0)]
    all_to_all x5 -> x3, waiting for transfers between devices: 48.8 us -> 18.2 us  [spread_rows(): return lax.all_to_all(pieces, axes, 0, 0)]
    all_gather x0 -> x1, blocking collectives: none -> 9.62 us  [on_device(): packed = lax.all_gather(packed, 'ffn', axis=0, tiled=False)]
    ppermute x2, waiting for transfers between devices: 10 us -> 2.16 us  [passed_along(): lax.ppermute(rows, AXES, [(i, (i + by) % peers) for i in range(peers)])]
    unnamed x20 -> x10, local copies, waits for them, and re-layouts: 6.08 us -> 2.18 us
    ppermute x2, starting transfers between devices: 1.05 us -> 4.28 us  [passed_along(): lax.ppermute(rows, AXES, [(i, (i + by) % peers) for i in range(peers)])]
    all_to_all x5 -> x3, starting transfers between devices: 14.7 us -> 14.2 us  [spread_rows(): return lax.all_to_all(pieces, axes, 0, 0)]
  transfers between devices with their start and end apart: 7 -> 5, of which waited for: 7 -> 2; matrix products, arithmetic and copies ran while one was open for 0% -> 0% of each run, Pallas kernels for 5% -> 22%
where the time goes in v2:
time: 175 us; the launch traced here: 174 us
  Pallas kernels  87.5 us (50%)
  blocking collectives  45 us (26%)
  waiting for transfers between devices  20.3 us (12%)
  starting transfers between devices  18.5 us (11%)
  local copies, waits for them, and re-layouts  2.18 us (1%)
    all_to_all x2, blocking collectives, spread_rows(): return lax.all_to_all(pieces, axes, 0, 0)  35.4 us
    pallas_call x1, Pallas kernels, on_device(): pl.pallas_call(functools.partial(second_back_kernel, ffns=ffns), grid=(st...  20.9 us
    all_to_all x3, waiting for transfers between devices, spread_rows(): return lax.all_to_all(pieces, axes, 0, 0)  18.2 us
    pallas_call x1, Pallas kernels, on_device(): pl.pallas_call(second_kernel, grid=(steps,), in_specs=[whole(row_count, W...  15.6 us
    pallas_call x1, Pallas kernels, on_device(): pl.pallas_call(functools.partial(first_attention_back_kernel, ffns=ffns),...  15.3 us
    all_to_all x3, starting transfers between devices, spread_rows(): return lax.all_to_all(pieces, axes, 0, 0)  14.2 us
    all_gather x1, blocking collectives, on_device(): packed = lax.all_gather(packed, 'ffn', axis=0, tiled=False)  9.62 us
    pallas_call x1, Pallas kernels, on_device(): pl.pallas_call(functools.partial(first_kernel, tail=True), grid=(steps -...  9.31 us
  transfers between devices with their start and end apart: 5, of which 2 were waited for; matrix products, arithmetic and copies ran while one was open for 0% of the time, Pallas kernels for 22%

profile of v2, /device:TPU:0, one launch (start us, length us, event | category | flops | bytes accessed | tf_op | source)
XLA Modules:
  0.0 174.4 jit_solution(6301084393606564773)
XLA Ops:
  0.6 2.8 %vfe.1 = (f32[864,128]{1,0:T(8,128)}, f32[864,1]{1,0:T(8,128)}, f32[32,8,128]{2,1,0:T(8,128)}, f32[264,128]{1,0:T(8,128)}) custom-call(f32[864,128]{1,0:T(8,128)} %feats_ref.3, f32[128,128]{1,0:T(8,128)} %weight_ref.3, s32[864]{0:T(1024)} %occupied_ref.1, f32[2,64,128]{2,1,0:T(8,128)} %bitcast.9, f32[2,64,128]{2,1,0:T(8,128)} %down_ref.1, f32[2,64]{1,0:T(2,128)} %bias_ref.1), custom_call_target="tpu_custom_call" | custom-call | tf_op jit(solution)/shard_map/vfe/pallas_call | solution.py:918
  3.4 7.3 %all-to-all-start = ((f32[32,8,128]{2,1,0:T(8,128)}), f32[32,8,128]{2,1,0:T(8,128)S(1)}, u32[]{:S(2)}, u32[]{:S(2)}) async-start(f32[32,8,128]{2,1,0:T(8,128)} %get-tuple-element.113), calls=%async_computation | async-start | bytes 262144 | tf_op jit(solution)/shard_map/all_to_all | solution.py:875
  10.8 1.9 %split.1 = (bf16[2,128,384]{2,1,0:T(8,128)(2,1)}, bf16[2,128,384]{2,1,0:T(8,128)(2,1)}, bf16[2,128,128]{2,1,0:T(8,128)(2,1)}, bf16[2,128,128]{2,1,0:T(8,128)(2,1)}) custom-call(f32[2,128,384]{2,1,0:T(8,128)} %qkv_ref.1, f32[2,128,128]{2,1,0:T(8,128)} %out_ref.1), custom_call_target="tpu_custom_call" | custom-call | flops 1000000 | bytes 1000000 | tf_op jit(solution)/shard_map/split/pallas_call | solution.py:938
  12.6 9.6 %all-gather = f32[1056,128]{1,0:T(8,128)} all-gather(f32[264,128]{1,0:T(8,128)} %get-tuple-element.112), channel_id=2, replica_groups=mesh['win'=8,'ffn'=4] {'ffn'}, dimensions={0}, use_global_device_ids=true | all-gather | bytes 675840 | tf_op jit(solution)/shard_map/all_gather | solution.py:937
  22.2 0.0 all-to-all-done.refs_13_
  22.2 0.7 copy-done.2
  22.9 5.8 %first.1 = (f32[72,384]{1,0:T(8,128)}, f32[8,128]{1,0:T(8,128)}, f32[8,128]{1,0:T(8,128)}, f32[864,128]{1,0:T(8,128)}, f32[864,128]{1,0:T(8,128)}, /*index=5*/f3...) custom-call(f32[864,128]{1,0:T(8,128)} %get-tuple-element.106.refs_0, ...), custom_call_target="tpu_custom_call" | custom-call | flops 1000000000 | bytes 4000000 | tf_op jit(solution)/shard_map/first/pallas_call | solution.py:1005
  28.7 4.0 %collective-permute-start = (f32[72,384]{1,0:T(8,128)}, f32[72,384]{1,0:T(8,128)S(1)}, u32[]{:S(2)}, u32[]{:S(2)}) collective-permute-start(f32[72,384]{1,0:T(8,128)} %get-tuple-element.130), channel_id=1, source_target_pairs={{0,31},{1,0},{2,1},{3,2},{4,3},{5,4},{6,5},{7,6},{8,7},{9,8},{10,9... | collective-permute-start | bytes 331784 | tf_op jit(solution)/shard_map/ppermute | solution.py:880
  32.7 9.3 %first_rest.1 = (f32[864,128]{1,0:T(8,128)}, f32[864,128]{1,0:T(8,128)}, f32[864,128]{1,0:T(8,128)}, f32[864,128]{1,0:T(8,128)}, f32[864,384]{1,0:T(8,128)}, /*i...) custom-call(f32[864,128]{1,0:T(8,128)} %get-tuple-element.106.refs_0, ...), custom_call_target="tpu_custom_call", output_to_operand_aliasing={{0}: (13, {}), {1}: (14, {}), {2}: (15, {}), {3}: (16, {}),... | custom-call | flops 2000000000 | bytes 8000000 | tf_op jit(solution)/shard_map/first_rest/pallas_call | solution.py:1017
  42.1 0.0 collective-permute-done.edge
  42.1 0.0 copy-start.4
  42.1 0.6 copy-done.4
  42.7 15.6 %second.1 = (f32[864,128]{1,0:T(8,128)}, f32[32,8,128]{2,1,0:T(8,128)}, f32[864,1]{1,0:T(8,128)}, f32[864,128]{1,0:T(8,128)}, f32[864,128]{1,0:T(8,128)}, /*inde...) custom-call(f32[864,128]{1,0:T(8,128)} %get-tuple-element.129.first_, ...), custom_call_target="tpu_custom_call" | custom-call | flops 4000000000 | bytes 12000000 | tf_op jit(solution)/shard_map/second/pallas_call | solution.py:1033
  58.3 11.5 %all_to_all.25.seen_ref = f32[32,8,128]{2,1,0:T(8,128)} all-to-all(f32[32,8,128]{2,1,0:T(8,128)} %get-tuple-element.132), channel_id=1, replica_groups=mesh['win'=8,'ffn'=4] {'win','ffn'}, dimensions={0} | all-to-all | bytes 262144 | tf_op jit(solution)/shard_map/all_to_all | solution.py:875
  69.8 20.9 %second_back.1 = (f32[32,32,128]{2,1,0:T(8,128)}, f32[72,256]{1,0:T(8,128)}, f32[864,128]{1,0:T(8,128)}, f32[864,128]{1,0:T(8,128)}, f32[8,128]{1,0:T(8,128)}, /*index=5*/f32[8,128]{1,0:T(8,128)}) custom-call(f32[864,128]{1,0:T(8,128)} %get-tuple-element.131.result, f32[32,8,128]{2,1,0:T(8,128)} %all_to_all.25.seen_ref, f32[2,128]{1,0:T(2,128)} %bn_gain.5, ...), custom_call_target="tpu_custom_call" | custom-call | flops 8000000000 | bytes 12000000 | tf_op jit(solution)/shard_map/second_back/pallas_call | solution.py:1082
  90.7 0.3 collective-permute-start.1
  91.0 5.2 %first_ffn_back.1 = (f32[864,128]{1,0:T(8,128)}, f32[864,128]{1,0:T(8,128)}, f32[8,128]{1,0:T(8,128)}, f32[128,128]{1,0:T(8,128)}, f32[256,128]{1,0:T(8,128)}, /*index=5*/f32[256,128]{1,0:T(8,128)}) custom-call(f32[864,128]{1,0:T(8,128)} %get-tuple-element.146.refs_0_, bf16[2,128,128]{2,1,0:T(8,128)(2,1)} %get-tuple-element.110.refs_6_.out_high.refs_1_, ...), custom_call_target="tpu_custom_call" | custom-call | flops 2000000000 | bytes 4000000 | tf_op jit(solution)/shard_map/first_ffn_back/pallas_call | solution.py:1138
  96.2 2.2 %collective-permute-done.1.refs_13_ = f32[72,256]{1,0:T(8,128)S(1)} collective-permute-done((f32[72,256]{1,0:T(8,128)}, f32[72,256]{1,0:T(8,128)S(1)}, u32[]{:S(2)}, u32[]{:S(2)}) %collective-permute-start.1) | collective-permute-done | bytes 73760 | tf_op jit(solution)/shard_map/ppermute | solution.py:880
  98.3 3.4 %all-to-all-start.2 = ((f32[32,32,128]{2,1,0:T(8,128)}), f32[32,32,128]{2,1,0:T(8,128)S(1)}, u32[]{:S(2)}, u32[]{:S(2)}) async-start(f32[32,32,128]{2,1,0:T(8,128)} %get-tuple-element.180), calls=%async_computation.2 | async-start | bytes 1048576 | tf_op jit(solution)/shard_map/all_to_all | solution.py:875
  101.7 0.0 copy-done.3
  101.7 3.7 %first_ffn_back_edge.1 = (f32[864,128]{1,0:T(8,128)}, f32[864,128]{1,0:T(8,128)}, f32[864,128]{1,0:T(8,128)}, f32[8,128]{1,0:T(8,128)}, f32[128,128]{1,0:T(8,128...) custom-call(f32[864,128]{1,0:T(8,128)} %get-tuple-element.146.refs_0_, ...), custom_call_target="tpu_custom_call", output_to_operand_aliasing={{2}: (14, {}), {0}: (19, {}), {1}: (20, {})} | custom-call | flops 1000000000 | bytes 2000000 | tf_op jit(solution)/shard_map/first_ffn_back_edge/pallas_call | solution.py:1153
  105.5 15.3 %first_attention_back.1 = (f32[864,128]{1,0:T(8,128)}, f32[32,40,128]{2,1,0:T(8,128)}) custom-call(f32[864,128]{1,0:T(8,128)} %get-tuple-element.166.grad_joined, f32[864,128]{1,0:T(8,128)} %get-tuple-element.167.grad_mixed, f32[864,128]{1,0:T(8,128)} %feats_ref.3, f32[864,1]{1,0:T(8,128)} %get-tuple-element.107.refs_1_.live_ref, ...), custom_call_target="tpu_custom_call" | custom-call | flops 6000000000 | bytes 8000000 | tf_op jit(solution)/shard_map/first_attention_back/pallas_call | solution.py:1168
  120.8 0.0 all-to-all-done.2.early
  120.8 0.0 copy-start.1
  120.8 23.9 %all_to_all.26.late = f32[32,40,128]{2,1,0:T(8,128)} all-to-all(f32[32,40,128]{2,1,0:T(8,128)} %get-tuple-element.183), channel_id=1, replica_groups=mesh['win'=8,'ffn'=4] {'win','ffn'}, dimensions={0} | all-to-all | bytes 1310720 | tf_op jit(solution)/shard_map/all_to_all | solution.py:875
  144.7 0.0 copy-done.1
  144.7 2.3 %relay.1 = (f32[32,48,128]{2,1,0:T(8,128)}, f32[8,128]{1,0:T(8,128)}) custom-call(f32[32,32,128]{2,1,0:T(8,128)} %copy-done.1, f32[32,40,128]{2,1,0:T(8,128)} %all_to_all.26.late, f32[8,128]{1,0:T(8,128)} %get-tuple-element.184.hat_product, f32[8,128]{1,0:T(8,128)} %get-tuple-element.114.refs_12_.stats, f32[2,128]{1,0:T(2,128)} %bn_gain.5), custom_call_target="tpu_custom_call" | custom-call | tf_op jit(solution)/shard_map/relay/pallas_call | solution.py:1200
  147.0 3.5 %all-to-all-start.4 = ((f32[32,48,128]{2,1,0:T(8,128)}), f32[32,48,128]{2,1,0:T(8,128)S(1)}, u32[]{:S(2)}, u32[]{:S(2)}) async-start(f32[32,48,128]{2,1,0:T(8,128)} %get-tuple-element.186), calls=%async_computation.4 | async-start | bytes 1572864 | tf_op jit(solution)/shard_map/all_to_all | solution.py:875
  150.5 2.5 %feats_back.1 = f32[864,128]{1,0:T(8,128)} custom-call(f32[864,128]{1,0:T(8,128)} %get-tuple-element.179.grad_affine, f32[864,128]{1,0:T(8,128)} %get-tuple-element.169.vfe_hat, f32[864,1]{1,0:T(8,128)} %get-tuple-element.107.refs_1_.live_ref, f32[8,128]{1,0:T(8,128)} %get-tuple-element.114.refs_12_.stats, f32[8,128]{1,0:T(8,128)} %get-tuple-element.185.vfe_grads, ...), custom_call_target="tpu_custom_call" | custom-call | flops 100000000 | bytes 2000000 | tf_op jit(solution)/shard_map/feats_back/pallas_call | solution.py:1207
  152.9 18.2 %all-to-all-done.4.returned = f32[32,48,128]{2,1,0:T(8,128)S(1)} async-done(((f32[32,48,128]{2,1,0:T(8,128)}), f32[32,48,128]{2,1,0:T(8,128)S(1)}, u32[]{:S(2)}, u32[]{:S(2)}) %all-to-all-start.4) | async-done | bytes 786464 | tf_op jit(solution)/shard_map/all_to_all | solution.py:875
  171.1 0.9 copy-done
  172.0 2.3 %last.1 = (f32[128,128]{1,0:T(8,128)}, f32[2,128]{1,0:T(2,128)}, f32[2,128]{1,0:T(2,128)}, f32[2,128,384]{2,1,0:T(8,128)}, f32[2,128,128]{2,1,0:T(8,128)}, /*ind...) custom-call(f32[32,48,128]{2,1,0:T(8,128)} %copy-done, ...), custom_call_target="tpu_custom_call" | custom-call | tf_op jit(solution)/shard_map/last/pallas_call | solution.py:1214
  (3 shorter events, 0.0 us)
Async XLA Ops:
  3.4 18.8 %all-to-all-start = ((f32[32,8,128]{2,1,0:T(8,128)}), f32[32,8,128]{2,1,0:T(8,128)S(1)}, u32[]{:S(2)}, u32[]{:S(2)}) async-start(f32[32,8,128]{2,1,0:T(8,128)} %get-tuple-element.113), calls=%async_computation | async-start | bytes 262144 | tf_op jit(solution)/shard_map/all_to_all | solution.py:875
  22.2 0.7 copy-start.2
  28.7 13.3 %collective-permute-start = (f32[72,384]{1,0:T(8,128)}, f32[72,384]{1,0:T(8,128)S(1)}, u32[]{:S(2)}, u32[]{:S(2)}) collective-permute-start(f32[72,384]{1,0:T(8,128)} %get-tuple-element.130), channel_id=1, source_target_pairs={{0,31},{1,0},{2,1},{3,2},{4,3},{5,4},{6,5},{7,6},{8,7},{9,8},{10,9... | collective-permute-start | bytes 331784 | tf_op jit(solution)/shard_map/ppermute | solution.py:880
  42.1 0.6 copy-start.4
  90.7 7.6 %collective-permute-start.1 = (f32[72,256]{1,0:T(8,128)}, f32[72,256]{1,0:T(8,128)S(1)}, u32[]{:S(2)}, u32[]{:S(2)}) collective-permute-start(f32[72,256]{1,0:T(8,128)} %get-tuple-element.155), channel_id=1, source_target_pairs={{0,1},{1,2},{2,3},{3,4},{4,5},{5,6},{6,7},{7,8},{8,9},{9,10},{10,1... | collective-permute-start | bytes 221192 | tf_op jit(solution)/shard_map/ppermute | solution.py:880
  98.3 3.4 %copy-start.3 = (f32[72,256]{1,0:T(8,128)}, f32[72,256]{1,0:T(8,128)S(1)}, u32[]{:S(2)}) copy-start(f32[72,256]{1,0:T(8,128)S(1)} %collective-permute-done.1.refs_13_) | copy-start | bytes 221188
  98.3 22.4 %all-to-all-start.2 = ((f32[32,32,128]{2,1,0:T(8,128)}), f32[32,32,128]{2,1,0:T(8,128)S(1)}, u32[]{:S(2)}, u32[]{:S(2)}) async-start(f32[32,32,128]{2,1,0:T(8,128)} %get-tuple-element.180), calls=%async_computation.2 | async-start | bytes 1048576 | tf_op jit(solution)/shard_map/all_to_all | solution.py:875
  120.8 23.9 %copy-start.1 = (f32[32,32,128]{2,1,0:T(8,128)}, f32[32,32,128]{2,1,0:T(8,128)S(1)}, u32[]{:S(2)}) copy-start(f32[32,32,128]{2,1,0:T(8,128)S(1)} %all-to-all-done.2.early) | copy-start | bytes 1572868
  147.0 24.1 %all-to-all-start.4 = ((f32[32,48,128]{2,1,0:T(8,128)}), f32[32,48,128]{2,1,0:T(8,128)S(1)}, u32[]{:S(2)}, u32[]{:S(2)}) async-start(f32[32,48,128]{2,1,0:T(8,128)} %get-tuple-element.186), calls=%async_computation.4 | async-start | bytes 1572864 | tf_op jit(solution)/shard_map/all_to_all | solution.py:875
  171.1 0.9 copy-start
